TPU v7x, 32 devices: a whole 2x2x4 slice. The times are simulated.
32 devices in a mesh: dp: 32 (over z, y, x, core).
Axes of the slice: x: 2, y: 2, z: 4, core: 2. Of those that a mesh axis runs over, the one named last changes fastest.
Arguments:
- inputs: bfloat16 [3, 32768, 384], P(None, 'dp'), may hold values from -6 to 6
- cotangent: bfloat16 [3, 32768, 384], P(None, 'dp'), may hold values from -6 to 6
- w_qkv: bfloat16 [384, 1152], P('dp'), may hold values from -0.3125 to 0.3125
- w_out: bfloat16 [384, 384], P('dp'), may hold values from -0.875 to 0.875
- w_fc1: bfloat16 [384, 1536], P('dp'), may hold values from -0.3125 to 0.3125
- w_fc2: bfloat16 [1536, 384], P('dp'), may hold values from -0.15625 to 0.15625
- norm1_gain: bfloat16 [384], P('dp'), may hold values from 0.5 to 1.5
- norm1_bias: bfloat16 [384], P('dp'), may hold values from -4 to 4
- query_bias: bfloat16 [384], P('dp'), may hold values from -6 to 6
- value_bias: bfloat16 [384], P('dp'), may hold values from -6 to 6
- out_bias: bfloat16 [384], P('dp'), may hold values from -4 to 4
- norm2_gain: bfloat16 [384], P('dp'), may hold values from 0.5 to 1.5
- norm2_bias: bfloat16 [384], P('dp'), may hold values from -4 to 4
- fc1_bias: bfloat16 [1536], P('dp'), may hold values from -6 to 6
- fc2_bias: bfloat16 [384], P('dp'), may hold values from -4 to 4
- image_tokens: int32 [3, 32], replicated, may hold values from 102 to 326, as said below
- image_count: int32 [3, 32], replicated, may hold values from 2 to 10, as said below
Outputs:
- outputs: bfloat16 [3, 32768, 384], P(None, 'dp')
- input_grad: bfloat16 [3, 32768, 384], P(None, 'dp')
- grad_qkv: float32 [384, 1152], P('dp')
- grad_out: float32 [384, 384], P('dp')
- grad_fc1: float32 [384, 1536], P('dp')
- grad_fc2: float32 [1536, 384], P('dp')
- grad_norm1_gain: float32 [384], P('dp')
- grad_norm1_bias: float32 [384], P('dp')
- grad_query_bias: float32 [384], P('dp')
- grad_value_bias: float32 [384], P('dp')
- grad_out_bias: float32 [384], P('dp')
- grad_norm2_gain: float32 [384], P('dp')
- grad_norm2_bias: float32 [384], P('dp')
- grad_fc1_bias: float32 [1536], P('dp')
- grad_fc2_bias: float32 [384], P('dp')
Inputs may be any that keep to these rules, and one draw needn't show every extreme that they name: `image_tokens`: each entry is one of 102, 198, 326. image_count times the matching image_tokens entry is at most 1024; the images fill the first slots of their block.
All inputs are finite; a program needn't handle non-finite values.
Results may differ from a plain program's by a relative error of at most 0.012.
Values may be sent and summed in bfloat16 or wider, within the bound.
A program may use at most 192 MiB of HBM per device.

v0:
```python
import jax
import jax.numpy as jnp
from jax import lax
from jax.sharding import PartitionSpec as P

HEADS = 6


norm_eps = 1e-06
masked_score = -1000000000.0


def from_partner(array, axis, bit):
    return lax.ppermute(array, axis, [(i, i ^ 1 << bit) for i in range(lax.axis_size(axis))])


def normalize(values, gain, shift):
    center = jnp.mean(values, axis=-1, keepdims=True)
    offset = values - center
    spread = jnp.mean(offset * offset, axis=-1, keepdims=True)
    return offset * lax.rsqrt(spread + norm_eps) * gain + shift


def smooth_gate(values):
    return jax.nn.gelu(values, approximate=False)


def segments(length, count, row_count):
    places = jnp.arange(row_count, dtype=jnp.int32)
    image_of = places // length
    valid = image_of < count
    return (jnp.where(valid, image_of, row_count + places), valid)


def over_rows(left, right):
    return lax.dot_general(
        left, right, (((0,), (0,)), ((), ())), preferred_element_type=jnp.float32
    )


def against(left, right):
    return lax.dot_general(
        left, right, (((1,), (1,)), ((), ())), preferred_element_type=jnp.float32
    )


def block_scores(query_block, keys, seg_block, segment_ids, scale):
    scores = (
        jnp.einsum("qhd,khd->hqk", query_block, keys, preferred_element_type=jnp.float32) * scale
    )
    same_image = seg_block[:, None] == segment_ids[None, :]
    return jnp.where(same_image[None], scores, masked_score)


def attend(queries, keys, values, segment_ids, scale):
    row_count = queries.shape[0]
    block_rows = min(512, row_count)

    def one_block(block_index):
        start = block_index * block_rows
        query_block = lax.dynamic_slice_in_dim(queries, start, block_rows, 0)
        seg_block = lax.dynamic_slice_in_dim(segment_ids, start, block_rows, 0)
        scores = block_scores(query_block, keys, seg_block, segment_ids, scale)
        highest = jnp.max(scores, axis=-1, keepdims=True)
        raised = jnp.exp(scores - highest)
        totals = jnp.sum(raised, axis=-1, keepdims=True)
        weights = (raised / totals).astype(jnp.bfloat16)
        result = jnp.einsum("hqk,khd->qhd", weights, values, preferred_element_type=jnp.float32)
        return (result.astype(jnp.bfloat16), (highest + jnp.log(totals))[..., 0])

    results, log_sums = lax.map(one_block, jnp.arange(row_count // block_rows))
    return (results.reshape(row_count, -1), log_sums)


def attend_back(queries, keys, values, segment_ids, log_sums, grad_heads, scale):
    row_count, head_count, head_dim = queries.shape
    block_rows = min(512, row_count)

    def one_block(carry, block_index):
        grad_keys, grad_values = carry
        start = block_index * block_rows
        query_block = lax.dynamic_slice_in_dim(queries, start, block_rows, 0)
        seg_block = lax.dynamic_slice_in_dim(segment_ids, start, block_rows, 0)
        grad_block = lax.dynamic_slice_in_dim(grad_heads, start, block_rows, 0)
        scores = block_scores(query_block, keys, seg_block, segment_ids, scale)
        weights = jnp.exp(scores - log_sums[block_index][..., None])
        grad_weights = jnp.einsum(
            "qhd,khd->hqk", grad_block, values, preferred_element_type=jnp.float32
        )
        inner = jnp.sum(weights * grad_weights, axis=-1, keepdims=True)
        grad_scores = (weights * (grad_weights - inner)).astype(jnp.bfloat16)
        grad_query = (
            jnp.einsum("hqk,khd->qhd", grad_scores, keys, preferred_element_type=jnp.float32)
            * scale
        )
        grad_keys = (
            grad_keys
            + jnp.einsum(
                "hqk,qhd->khd", grad_scores, query_block, preferred_element_type=jnp.float32
            )
            * scale
        )
        grad_values = grad_values + jnp.einsum(
            "hqk,qhd->khd",
            weights.astype(jnp.bfloat16),
            grad_block,
            preferred_element_type=jnp.float32,
        )
        return ((grad_keys, grad_values), grad_query)

    empty = jnp.zeros((row_count, head_count, head_dim), jnp.float32)
    (grad_keys, grad_values), grad_queries = lax.scan(
        one_block, (empty, empty), jnp.arange(row_count // block_rows)
    )
    return (grad_queries.reshape(row_count, head_count, head_dim), grad_keys, grad_values)


def own_pieces(full, first_head, head_count, head_dim):
    (
        w_qkv,
        w_out,
        w_fc1,
        w_fc2,
        norm1_gain,
        norm1_bias,
        query_bias,
        value_bias,
        out_bias,
        norm2_gain,
        norm2_bias,
        fc1_bias,
        fc2_bias,
    ) = full
    width = w_out.shape[1]
    heads_all = width // head_dim
    qkv_mine = lax.dynamic_slice_in_dim(
        w_qkv.reshape(width, 3, heads_all, head_dim), first_head, head_count, 2
    )
    qkv_mine = qkv_mine.reshape(width, 3 * head_count * head_dim)
    out_mine = lax.dynamic_slice_in_dim(
        w_out.reshape(heads_all, head_dim, width), first_head, head_count, 0
    )
    out_mine = out_mine.reshape(head_count * head_dim, width)
    bias_all = jnp.stack([query_bias, jnp.zeros_like(query_bias), value_bias]).astype(jnp.float32)
    bias_mine = lax.dynamic_slice_in_dim(
        bias_all.reshape(3, heads_all, head_dim), first_head, head_count, 1
    )
    vectors = tuple(
        (
            vector_item.astype(jnp.float32)
            for vector_item in (
                norm1_gain,
                norm1_bias,
                out_bias,
                norm2_gain,
                norm2_bias,
                fc1_bias,
                fc2_bias,
            )
        )
    )
    return (qkv_mine, out_mine, bias_mine.reshape(-1), w_fc1, w_fc2, vectors)


def body(
    inputs,
    cotangent,
    w_qkv,
    w_out,
    w_fc1,
    w_fc2,
    norm1_gain,
    norm1_bias,
    query_bias,
    value_bias,
    out_bias,
    norm2_gain,
    norm2_bias,
    fc1_bias,
    fc2_bias,
    image_tokens,
    image_count,
):
    shards = (
        w_qkv,
        w_out,
        w_fc1,
        w_fc2,
        norm1_gain,
        norm1_bias,
        query_bias,
        value_bias,
        out_bias,
        norm2_gain,
        norm2_bias,
        fc1_bias,
        fc2_bias,
    )
    micro_count, row_count, width = inputs.shape
    hidden = w_fc1.shape[1]
    head_dim = width // HEADS
    scale = head_dim ** (-0.5)
    position = lax.axis_index("dp")
    head_count = HEADS // 2
    first_head = position % 2 * head_count
    partner = position + 1 - 2 * (position % 2)
    part_width = head_count * head_dim
    acc_qkv = jnp.zeros((width, 3, HEADS, head_dim), jnp.float32)
    acc_out = jnp.zeros((HEADS, head_dim, width), jnp.float32)
    acc_fc1 = jnp.zeros((width, hidden), jnp.float32)
    acc_fc2 = jnp.zeros((hidden, width), jnp.float32)
    acc_bias_qkv = jnp.zeros((3, HEADS, head_dim), jnp.float32)
    acc_gain_one = jnp.zeros((width,), jnp.float32)
    acc_shift_one = jnp.zeros((width,), jnp.float32)
    acc_out_bias = jnp.zeros((width,), jnp.float32)
    acc_gain_two = jnp.zeros((width,), jnp.float32)
    acc_shift_two = jnp.zeros((width,), jnp.float32)
    acc_fc1_bias = jnp.zeros((hidden,), jnp.float32)
    acc_fc2_bias = jnp.zeros((width,), jnp.float32)
    layer_results = []
    input_grads = []
    for micro_step in range(micro_count):
        full = (
            lax.all_gather(shards[0], "dp", axis=0, tiled=True),
            lax.all_gather(shards[1], "dp", axis=0, tiled=True),
            lax.all_gather(shards[2], "dp", axis=0, tiled=True),
            lax.all_gather(shards[3], "dp", axis=0, tiled=True),
            lax.all_gather(shards[4], "dp", axis=0, tiled=True),
            lax.all_gather(shards[5], "dp", axis=0, tiled=True),
            lax.all_gather(shards[6], "dp", axis=0, tiled=True),
            lax.all_gather(shards[7], "dp", axis=0, tiled=True),
            lax.all_gather(shards[8], "dp", axis=0, tiled=True),
            lax.all_gather(shards[9], "dp", axis=0, tiled=True),
            lax.all_gather(shards[10], "dp", axis=0, tiled=True),
            lax.all_gather(shards[11], "dp", axis=0, tiled=True),
            lax.all_gather(shards[12], "dp", axis=0, tiled=True),
        )
        qkv_mine, out_mine, bias_mine, fc1_full, fc2_full, vectors = own_pieces(
            full, first_head, head_count, head_dim
        )
        gain_one, shift_one, bias_out, gain_two, shift_two, bias_fc1, bias_fc2 = vectors
        states = inputs[micro_step].astype(jnp.float32)
        own_ids, valid = segments(
            image_tokens[micro_step, position], image_count[micro_step, position], row_count
        )
        normed, norm_one_back = jax.vjp(normalize, states, gain_one, shift_one)
        normed_low = normed.astype(jnp.bfloat16)
        partner_rows = from_partner(normed_low, "dp", 0)
        partner_ids = segments(
            image_tokens[micro_step, partner], image_count[micro_step, partner], row_count
        )[0]
        both_rows = jnp.stack([normed_low, partner_rows])
        both_ids = [own_ids, partner_ids]
        buffer_count = len(both_ids)
        flat_rows = both_rows.reshape(buffer_count * row_count, width)
        qkv_low = (
            jnp.dot(flat_rows, qkv_mine, preferred_element_type=jnp.float32) + bias_mine
        ).astype(jnp.bfloat16)
        qkv_low = qkv_low.reshape(buffer_count, row_count, 3, head_count, head_dim)
        attended_list = []
        log_list = []
        for buffer_index in range(buffer_count):
            result, log_sums = attend(
                qkv_low[buffer_index, :, 0],
                qkv_low[buffer_index, :, 1],
                qkv_low[buffer_index, :, 2],
                both_ids[buffer_index],
                scale,
            )
            attended_list.append(result)
            log_list.append(log_sums)
        attended = jnp.stack(attended_list).reshape(buffer_count * row_count, part_width)
        partial_out = jnp.dot(attended, out_mine, preferred_element_type=jnp.float32)
        partial_out = partial_out.reshape(buffer_count, row_count, width)
        branch = partial_out[0] + from_partner(partial_out[1], "dp", 0)
        mixed = states + branch + bias_out
        normed_two, norm_two_back = jax.vjp(normalize, mixed, gain_two, shift_two)
        normed_two_low = normed_two.astype(jnp.bfloat16)
        pre_act = jnp.dot(normed_two_low, fc1_full, preferred_element_type=jnp.float32) + bias_fc1
        activated, gate_back = jax.vjp(smooth_gate, pre_act)
        activated_low = activated.astype(jnp.bfloat16)
        final = (
            mixed + jnp.dot(activated_low, fc2_full, preferred_element_type=jnp.float32) + bias_fc2
        )
        layer_results.append(jnp.where(valid[:, None], final, 0.0).astype(jnp.bfloat16))
        full = (
            lax.all_gather(shards[0], "dp", axis=0, tiled=True),
            lax.all_gather(shards[1], "dp", axis=0, tiled=True),
            lax.all_gather(shards[2], "dp", axis=0, tiled=True),
            lax.all_gather(shards[3], "dp", axis=0, tiled=True),
            lax.all_gather(shards[4], "dp", axis=0, tiled=True),
            lax.all_gather(shards[5], "dp", axis=0, tiled=True),
            lax.all_gather(shards[6], "dp", axis=0, tiled=True),
            lax.all_gather(shards[7], "dp", axis=0, tiled=True),
            lax.all_gather(shards[8], "dp", axis=0, tiled=True),
            lax.all_gather(shards[9], "dp", axis=0, tiled=True),
            lax.all_gather(shards[10], "dp", axis=0, tiled=True),
            lax.all_gather(shards[11], "dp", axis=0, tiled=True),
            lax.all_gather(shards[12], "dp", axis=0, tiled=True),
        )
        qkv_mine, out_mine, bias_mine, fc1_full, fc2_full, vectors = own_pieces(
            full, first_head, head_count, head_dim
        )
        grad_final = jnp.where(valid[:, None], cotangent[micro_step].astype(jnp.float32), 0.0)
        grad_final_low = grad_final.astype(jnp.bfloat16)
        acc_fc2_bias = acc_fc2_bias + jnp.sum(grad_final, axis=0)
        acc_fc2 = acc_fc2 + over_rows(activated_low, grad_final_low)
        (grad_pre,) = gate_back(against(grad_final_low, fc2_full))
        grad_pre_low = grad_pre.astype(jnp.bfloat16)
        acc_fc1_bias = acc_fc1_bias + jnp.sum(grad_pre_low, axis=0, dtype=jnp.float32)
        acc_fc1 = acc_fc1 + over_rows(normed_two_low, grad_pre_low)
        grad_mixed_norm, grad_gain_two, grad_shift_two = norm_two_back(
            against(grad_pre_low, fc1_full)
        )
        acc_gain_two = acc_gain_two + grad_gain_two
        acc_shift_two = acc_shift_two + grad_shift_two
        grad_mixed = grad_final + grad_mixed_norm
        grad_branch_low = grad_mixed.astype(jnp.bfloat16)
        acc_out_bias = acc_out_bias + jnp.sum(grad_branch_low, axis=0, dtype=jnp.float32)
        partner_grads = from_partner(grad_branch_low, "dp", 0)
        grad_both = jnp.stack([grad_branch_low, partner_grads])
        flat_grads = grad_both.reshape(buffer_count * row_count, width)
        out_piece = over_rows(attended, flat_grads).reshape(head_count, head_dim, width)
        acc_out = lax.dynamic_update_slice_in_dim(
            acc_out,
            lax.dynamic_slice_in_dim(acc_out, first_head, head_count, 0) + out_piece,
            first_head,
            0,
        )
        grad_heads = against(flat_grads, out_mine).astype(jnp.bfloat16)
        grad_heads = grad_heads.reshape(buffer_count, row_count, head_count, head_dim)
        qkv_grads = []
        for buffer_index in range(buffer_count):
            grad_query, grad_keys, grad_values = attend_back(
                qkv_low[buffer_index, :, 0],
                qkv_low[buffer_index, :, 1],
                qkv_low[buffer_index, :, 2],
                both_ids[buffer_index],
                log_list[buffer_index],
                grad_heads[buffer_index],
                scale,
            )
            qkv_grads.append(jnp.stack([grad_query, grad_keys, grad_values], axis=1))
        grad_qkv_low = jnp.stack(qkv_grads).astype(jnp.bfloat16)
        bias_piece = jnp.sum(grad_qkv_low, axis=(0, 1), dtype=jnp.float32)
        acc_bias_qkv = lax.dynamic_update_slice_in_dim(
            acc_bias_qkv,
            lax.dynamic_slice_in_dim(acc_bias_qkv, first_head, head_count, 1) + bias_piece,
            first_head,
            1,
        )
        flat_qkv = grad_qkv_low.reshape(buffer_count * row_count, 3 * part_width)
        qkv_piece = over_rows(flat_rows, flat_qkv).reshape(width, 3, head_count, head_dim)
        acc_qkv = lax.dynamic_update_slice_in_dim(
            acc_qkv,
            lax.dynamic_slice_in_dim(acc_qkv, first_head, head_count, 2) + qkv_piece,
            first_head,
            2,
        )
        partial_in = against(flat_qkv, qkv_mine).reshape(buffer_count, row_count, width)
        grad_normed = partial_in[0] + from_partner(
            partial_in[1].astype(jnp.bfloat16), "dp", 0
        ).astype(jnp.float32)
        grad_states, grad_gain_one, grad_shift_one = norm_one_back(grad_normed)
        acc_gain_one = acc_gain_one + grad_gain_one
        acc_shift_one = acc_shift_one + grad_shift_one
        input_grads.append((grad_mixed + grad_states).astype(jnp.bfloat16))
    summed = (
        lax.psum_scatter(acc_qkv.reshape(width, 3 * width), "dp", scatter_dimension=0, tiled=True),
        lax.psum_scatter(acc_out.reshape(width, width), "dp", scatter_dimension=0, tiled=True),
        lax.psum_scatter(acc_fc1, "dp", scatter_dimension=0, tiled=True),
        lax.psum_scatter(acc_fc2, "dp", scatter_dimension=0, tiled=True),
        lax.psum_scatter(acc_gain_one, "dp", scatter_dimension=0, tiled=True),
        lax.psum_scatter(acc_shift_one, "dp", scatter_dimension=0, tiled=True),
        lax.psum_scatter(acc_bias_qkv[0].reshape(width), "dp", scatter_dimension=0, tiled=True),
        lax.psum_scatter(acc_bias_qkv[2].reshape(width), "dp", scatter_dimension=0, tiled=True),
        lax.psum_scatter(acc_out_bias, "dp", scatter_dimension=0, tiled=True),
        lax.psum_scatter(acc_gain_two, "dp", scatter_dimension=0, tiled=True),
        lax.psum_scatter(acc_shift_two, "dp", scatter_dimension=0, tiled=True),
        lax.psum_scatter(acc_fc1_bias, "dp", scatter_dimension=0, tiled=True),
        lax.psum_scatter(acc_fc2_bias, "dp", scatter_dimension=0, tiled=True),
    )
    return (
        jnp.stack(layer_results),
        jnp.stack(input_grads),
        summed[0],
        summed[1],
        summed[2],
        summed[3],
        summed[4],
        summed[5],
        summed[6],
        summed[7],
        summed[8],
        summed[9],
        summed[10],
        summed[11],
        summed[12],
    )


def solution(mesh):
    return jax.shard_map(
        body,
        mesh=mesh,
        in_specs=(
            P(None, "dp", None),
            P(None, "dp", None),
            P("dp", None),
            P("dp", None),
            P("dp", None),
            P("dp", None),
            P("dp"),
            P("dp"),
            P("dp"),
            P("dp"),
            P("dp"),
            P("dp"),
            P("dp"),
            P("dp"),
            P("dp"),
            P(),
            P(),
        ),
        out_specs=(
            P(None, "dp", None),
            P(None, "dp", None),
            P("dp", None),
            P("dp", None),
            P("dp", None),
            P("dp", None),
            P("dp"),
            P("dp"),
            P("dp"),
            P("dp"),
            P("dp"),
            P("dp"),
            P("dp"),
            P("dp"),
            P("dp"),
        ),
        check_vma=False,
    )
```

profile of v0, /device:TPU:0, one launch (start us, length us, event | category | flops | bytes accessed | tf_op | source)
XLA Modules:
  0.0 1139.0 jit_solution(3212584496140996000)
XLA Ops:
  15.6 42.3 %all-reduce.25 = (bf16[384]{0:T(512)(128)(2,1)S(1)}, bf16[384]{0:T(512)(128)(2,1)S(1)}, bf16[384]{0:T(512)(128)(2,1)S(1)}, bf16[384]{0:T(512)(128)(2,1)S(1)}, bf...) all-reduce(bf16[384]{0:T(512)(128)(2,1)S(1)} %dynamic-update-slice., ...), channel_id=1, replica_groups=mesh['dp'=32] {'dp'}, use_global_device_ids=true, to_apply=%add.1 | all-reduce | flops 4608 | bytes 18432
  64.9 44.1 %all-gather = bf16[32,12,1152]{2,1,0:T(8,128)(2,1)S(1)} all-gather(bf16[1,12,1152]{2,1,0:T(8,128)(2,1)} %bitcast.846), channel_id=1, replica_groups=mesh['dp'=32] {'dp'}, dimensions={0}, use_global_device_ids=true | all-gather | bytes 912384 | tf_op jit(solution)/shard_map/all_gather | solution.py:224
  109.8 40.6 %all-gather.1 = bf16[32,12,384]{2,1,0:T(8,128)(2,1)} all-gather(bf16[1,12,384]{2,1,0:T(8,128)(2,1)} %bitcast.847), channel_id=1, replica_groups=mesh['dp'=32] {'dp'}, dimensions={0}, use_global_device_ids=true | all-gather | bytes 304128 | tf_op jit(solution)/shard_map/all_gather | solution.py:225
  195.3 17.6 %while.163 = (s32[]{:T(128)}, bf16[2,512,3,64]{1,3,2,0:T(8,128)(2,1)S(1)}, f32[2,3,512]{2,1,0:T(4,128)}, s32[2]{0:T(128)S(1)}, s32[1024]{0:T(1024)S(1)}, /*index...) while((s32[]{:T(128)}, ...), condition=%wide.region_9.10_spmd, body=%wide.region_6.9_spmd.sunk | while | flops 422148608 | bytes 22216904 | solution.py:71
  216.8 17.0 %while.162 = (s32[]{:T(128)}, bf16[2,512,3,64]{1,3,2,0:T(8,128)(2,1)}, f32[2,3,512]{2,1,0:T(4,128)}, s32[2]{0:T(128)S(1)}, s32[1024]{0:T(1024)S(1)}, /*index=5*/...) while((s32[]{:T(128)}, ...), condition=%wide.region_5.6_spmd, body=%wide.region_2.5_spmd.sunk | while | flops 422148608 | bytes 27038036 | solution.py:71
  257.1 17.1 %multiply_convert_fusion.8 = (bf16[1024,1536]{1,0:T(8,128)(2,1)}, f32[1024,1536]{1,0:T(8,128)}, f32[1024,1536]{1,0:T(8,128)}) fusion(f32[1536]{0:T(1024)S(1)} %convert_element_type.362, bf16[384,1536]{1,0:T(8,128)(2,1)S(1)} %copy-done.88, f32[1024,384]{1,0:T(8,128)S(1)} %get-tuple-element.1189, f32[384]{0:T(512)S(1)} %convert_element_type.360, ...), kind=kOutput, calls=%fused_computation.296 | convolution fusion | flops 1313734656 | bytes 18498560 | tf_op jit(solution)/shard_map/dot_general | solution.py:279
  274.2 26.1 %all-gather.6.cloned.1.call-done = bf16[1536,384]{1,0:T(8,128)(2,1)} async-done(((bf16[48,384]{1,0:T(8,128)(2,1)}), bf16[1536,384]{1,0:T(8,128)(2,1)}) %all-gather.6.cloned.1.call-update) | async-done | bytes 1179664 | tf_op jit(solution)/shard_map/all_gather | solution.py:227
  300.3 8.0 convert_reduce_fusion.2
  321.3 49.1 %while.169 = (s32[]{:T(128)}, f32[1024,3,64]{0,2,1:T(8,128)S(1)}, f32[1024,3,64]{0,2,1:T(8,128)}, bf16[2,512,3,64]{1,0,3,2:T(2,128)(2,1)}, s32[2]{0:T(128)S(1)},...) while((s32[]{:T(128)}, f32[1024,3,64]{0,2,1:T(8,128)S(1)}, ...), condition=%wide.region_43.44_spmd.clone, body=%wide.region_41.43_spmd.clone.sunk | while | flops 1031928320 | bytes 55431452 | solution.py:112
  338.2 7.6 dynamic_update_slice.148
  362.8 7.6 dynamic_update_slice.148
  373.4 39.8 %while.168 = (s32[]{:T(128)}, f32[1024,3,64]{0,2,1:T(8,128)S(1)}, f32[1024,3,64]{0,2,1:T(8,128)}, bf16[2,512,3,64]{1,0,3,2:T(2,128)(2,1)}, s32[2]{0:T(128)S(1)},...) while((s32[]{:T(128)}, f32[1024,3,64]{0,2,1:T(8,128)S(1)}, ...), condition=%wide.region_40.41_spmd.clone, body=%wide.region_38.40_spmd.clone.sunk | while | flops 1031928320 | bytes 61727116 | solution.py:112
  469.1 14.2 %while.164 = (s32[]{:T(128)}, bf16[2,512,3,64]{1,3,2,0:T(8,128)(2,1)S(1)}, f32[2,3,512]{2,1,0:T(4,128)S(1)}, s32[2]{0:T(128)S(1)}, s32[1024]{0:T(1024)S(1)}, /*i...) while((s32[]{:T(128)}, ...), condition=%wide.region_17.18_spmd, body=%wide.region_14.17_spmd.sunk | while | flops 422148608 | bytes 22221000 | solution.py:71
  487.0 17.8 %while.165 = (s32[]{:T(128)}, bf16[2,512,3,64]{1,3,2,0:T(8,128)(2,1)S(1)}, f32[2,3,512]{2,1,0:T(4,128)}, s32[2]{0:T(128)S(1)}, s32[1024]{0:T(1024)S(1)}, /*index...) while((s32[]{:T(128)}, ...), condition=%wide.region_21.22_spmd, body=%wide.region_18.21_spmd.sunk | while | flops 422148608 | bytes 22216904 | solution.py:71
  514.1 14.2 %while.166 = (s32[]{:T(128)}, bf16[2,512,3,64]{1,3,2,0:T(8,128)(2,1)S(1)}, f32[2,3,512]{2,1,0:T(4,128)S(1)}, s32[2]{0:T(128)S(1)}, s32[1024]{0:T(1024)S(1)}, /*i...) while((s32[]{:T(128)}, ...), condition=%wide.region_29.30_spmd, body=%wide.region_26.29_spmd.sunk | while | flops 422148608 | bytes 22221000 | solution.py:71
  531.2 17.6 %while.167 = (s32[]{:T(128)}, bf16[2,512,3,64]{1,3,2,0:T(8,128)(2,1)S(1)}, f32[2,3,512]{2,1,0:T(4,128)}, s32[2]{0:T(128)S(1)}, s32[1024]{0:T(1024)S(1)}, /*index...) while((s32[]{:T(128)}, ...), condition=%wide.region_33.34_spmd, body=%wide.region_30.33_spmd.sunk | while | flops 422148608 | bytes 22216904 | solution.py:71
  575.9 30.2 %multiply_convert_fusion.7 = (bf16[1024,1536]{1,0:T(8,128)(2,1)S(1)}, f32[1024,1536]{1,0:T(8,128)S(1)}, bf16[1024,1536]{1,0:T(8,128)(2,1)S(1)}, f32[1024,1536]{1,0:T(8,128)}, f32[1024,1536]{1,0:T(8,128)}) fusion(f32[1536]{0:T(1024)S(1)} %copy-done.208, f32[1024,1536]{1,0:T(8,128)S(1)} %fusion.354, bf16[384,1536]{1,0:T(8,128)(2,1)S(1)} %copy-done.90, ...), kind=kOutput, calls=%fused_computation.283 | convolution fusion | flops 1417543680 | bytes 34227200 | tf_op jit(solution)/shard_map/dot_general | solution.py:279
  606.1 8.4 convert_reduce_fusion
  655.6 49.1 %while.171 = (s32[]{:T(128)}, f32[1024,3,64]{0,2,1:T(8,128)S(1)}, f32[1024,3,64]{0,2,1:T(8,128)}, bf16[2,512,3,64]{1,0,3,2:T(2,128)(2,1)}, s32[2]{0:T(128)S(1)},...) while((s32[]{:T(128)}, f32[1024,3,64]{0,2,1:T(8,128)S(1)}, ...), condition=%wide.region_53.54_spmd.clone, body=%wide.region_51.53_spmd.clone.sunk | while | flops 1031928320 | bytes 55431452 | solution.py:112
  672.6 7.6 dynamic_update_slice.150
  697.1 7.6 dynamic_update_slice.150
  705.8 39.5 %while.170 = (s32[]{:T(128)}, f32[1024,3,64]{0,2,1:T(8,128)S(1)}, f32[1024,3,64]{0,2,1:T(8,128)}, bf16[2,512,3,64]{1,0,3,2:T(2,128)(2,1)}, s32[2]{0:T(128)S(1)},...) while((s32[]{:T(128)}, f32[1024,3,64]{0,2,1:T(8,128)S(1)}, ...), condition=%wide.region_50.51_spmd.clone, body=%wide.region_48.50_spmd.clone.sunk | while | flops 1031928320 | bytes 61727116 | solution.py:112
  752.7 49.4 %while.173 = (s32[]{:T(128)}, f32[1024,3,64]{0,2,1:T(8,128)S(1)}, f32[1024,3,64]{0,2,1:T(8,128)}, bf16[2,512,3,64]{1,0,3,2:T(2,128)(2,1)}, s32[2]{0:T(128)S(1)},...) while((s32[]{:T(128)}, f32[1024,3,64]{0,2,1:T(8,128)S(1)}, ...), condition=%wide.region_63.64_spmd.clone, body=%wide.region_61.63_spmd.clone.sunk | while | flops 1031928320 | bytes 55431452 | solution.py:112
  769.9 7.6 dynamic_update_slice.152
  794.5 7.6 dynamic_update_slice.152
  805.1 39.6 %while.172 = (s32[]{:T(128)}, f32[1024,3,64]{0,2,1:T(8,128)S(1)}, f32[1024,3,64]{0,2,1:T(8,128)}, bf16[2,512,3,64]{1,0,3,2:T(2,128)(2,1)}, s32[2]{0:T(128)S(1)},...) while((s32[]{:T(128)}, f32[1024,3,64]{0,2,1:T(8,128)S(1)}, ...), condition=%wide.region_60.61_spmd.clone, body=%wide.region_58.60_spmd.clone.sunk | while | flops 1031928320 | bytes 61727116 | solution.py:112
  873.8 82.4 %fusion.355 = (f32[16,1152]{1,0:T(8,128)S(1)}, f32[16,384]{1,0:T(8,128)S(1)}, f32[16,1536]{1,0:T(8,128)S(1)}) fusion(f32[384,1152]{1,0:T(8,128)S(1)} %copy-done.69, f32[384,384]{1,0:T(8,128)} %bitcast.820, f32[384,1536]{1,0:T(8,128)} %convolution_add_fusion.2), kind=kCustom, calls=%all-reduce-scatter.3 | all-reduce-scatter fusion | flops 1572865 | bytes 4915200
  973.8 8.4 collective-permute-start.21
  1011.7 12.5 %concatenate.2 = f32[140,384]{1,0:T(8,128)} concatenate(f32[12,384]{1,0:T(8,128)} %copy-done.190, f32[16,384]{1,0:T(8,128)S(1)} %collective-permute-done.26, f32[16,384]{1,0:T(8,128)S(1)} %collective-permute-done.25, f32[16,384]{1,0:T(8,128)} %copy-done.188, f32[16,384]{1,0:T(8,128)} %copy-done.189, f32[16,384]{1,0:T(8,128)} %collective-permute-done.22, ...), dimensions={0} | concatenate | bytes 430080
  1033.0 14.1 %concatenate.1 = f32[140,1152]{1,0:T(8,128)} concatenate(f32[12,1152]{1,0:T(8,128)} %collective-permute-done.19, f32[16,1152]{1,0:T(8,128)} %collective-permute-done.18, f32[16,1152]{1,0:T(8,128)} %collective-permute-done.17, f32[16,1152]{1,0:T(8,128)} %collective-permute-done.16, f32[16,1152]{1,0:T(8,128)} %collective-permute-done.15, f32[16,1152]{1,0:T(8,128)} %collective-permute-done.14, ...), dimensions={0} | concatenate | bytes 1290240
  1055.7 14.2 %concatenate.3 = f32[140,1536]{1,0:T(8,128)} concatenate(f32[12,1536]{1,0:T(8,128)} %collective-permute-done.35, f32[16,1536]{1,0:T(8,128)S(1)} %collective-permute-done.34, f32[16,1536]{1,0:T(8,128)} %collective-permute-done.33, f32[16,1536]{1,0:T(8,128)} %collective-permute-done.32, f32[16,1536]{1,0:T(8,128)} %collective-permute-done.31, ...), dimensions={0} | concatenate | bytes 1720320
  1084.0 39.1 %all-reduce.24 = (f32[384]{0:T(512)S(1)}, f32[384]{0:T(512)S(1)}, f32[384]{0:T(512)S(1)}, f32[384]{0:T(512)S(1)}, f32[384]{0:T(512)S(1)}, /*index=5*/f32[384]{0:...) all-reduce(f32[384]{0:T(512)S(1)} %add_add_fusion.12, ...), channel_id=6, replica_groups=mesh['dp'=32] {'dp'}, use_global_device_ids=true, to_apply=%region_73.74.clone | all-reduce | flops 4608 | bytes 36864
  (1076 shorter events, 641.8 us)
Async XLA Ops:
  7.2 243.1 %all-gather.8.cloned.1.call-start = ((), (), s32[]{:S(2)}) async-start(), calls=%async_computation.3 | async-start | bytes 1622016 | tf_op jit(solution)/shard_map/all_gather | solution.py:226
  7.9 292.4 %all-gather.6.cloned.1.call-start = ((), (), s32[]{:S(2)}) async-start(), calls=%async_computation.1 | async-start | bytes 1216512 | tf_op jit(solution)/shard_map/all_gather | solution.py:227
  63.5 110.2 %collective-permute-start = (bf16[1024,384]{1,0:T(8,128)(2,1)}, bf16[1024,384]{1,0:T(8,128)(2,1)}, u32[]{:S(2)}, u32[]{:S(2)}) collective-permute-start(bf16[1024,384]{1,0:T(8,128)(2,1)} %fusion.262), channel_id=1, source_target_pairs={{0,1},{1,0},{2,3},{3,2},{4,5},{5,4},{6,7},{7,6},{8,9},{9,8},{10,11... | collective-permute-start | bytes 2359304 | tf_op jit(solution)/shard_map/ppermute | solution.py:14
  248.7 883.3 %reduce-scatter.8.cloned.1.call-start = ((), (), s32[]{:S(2)}) async-start(), calls=%async_computation.2 | async-start | bytes 2433024 | tf_op jit(solution)/shard_map/reduce_scatter | solution.py:372
  436.4 10.6 collective-permute-start.4
  440.4 13.7 %collective-permute-start.2 = (bf16[1024,384]{1,0:T(8,128)(2,1)}, bf16[1024,384]{1,0:T(8,128)(2,1)}, u32[]{:S(2)}, u32[]{:S(2)}) collective-permute-start(bf16[1024,384]{1,0:T(8,128)(2,1)} %get-tuple-element.1216), channel_id=1, source_target_pairs={{0,1},{1,0},{2,3},{3,2},{4,5},{5,4},{6,7},{7,6},{8,9},{9,8},{10,11... | collective-permute-start | bytes 2359304 | tf_op jit(solution)/shard_map/ppermute | solution.py:14
  552.8 15.2 %collective-permute-start.5 = (f32[1024,384]{1,0:T(8,128)}, f32[1024,384]{1,0:T(8,128)}, u32[]{:S(2)}, u32[]{:S(2)}) collective-permute-start(f32[1024,384]{1,0:T(8,128)} %slice.238), channel_id=1, source_target_pairs={{0,1},{1,0},{2,3},{3,2},{4,5},{5,4},{6,7},{7,6},{8,9},{9,8},{10,11... | collective-permute-start | bytes 4718600 | tf_op jit(solution)/shard_map/ppermute | solution.py:14
  555.0 13.6 %collective-permute-start.3 = (f32[1024,384]{1,0:T(8,128)}, f32[1024,384]{1,0:T(8,128)}, u32[]{:S(2)}, u32[]{:S(2)}) collective-permute-start(f32[1024,384]{1,0:T(8,128)} %slice.230), channel_id=1, source_target_pairs={{0,1},{1,0},{2,3},{3,2},{4,5},{5,4},{6,7},{7,6},{8,9},{9,8},{10,11... | collective-permute-start | bytes 4718600 | tf_op jit(solution)/shard_map/ppermute | solution.py:14
  640.3 11.7 %collective-permute-start.8 = (bf16[1024,384]{1,0:T(8,128)(2,1)S(1)}, bf16[1024,384]{1,0:T(8,128)(2,1)S(1)}, u32[]{:S(2)}, u32[]{:S(2)}) collective-permute-start(bf16[1024,384]{1,0:T(8,128)(2,1)S(1)} %get-tuple-element.1155), channel_id=1, source_target_pairs={{0,1},{1,0},{2,3},{3,2},{4,5},{5,4},{6,7},{7,6},{8,9},{9,8},{10,11... | collective-permute-start | bytes 2359304 | tf_op jit(solution)/shard_map/ppermute | solution.py:14
  640.6 107.7 %collective-permute-start.10 = (bf16[1024,384]{1,0:T(8,128)(2,1)}, bf16[1024,384]{1,0:T(8,128)(2,1)}, u32[]{:S(2)}, u32[]{:S(2)}) collective-permute-start(bf16[1024,384]{1,0:T(8,128)(2,1)} %get-tuple-element.1225), channel_id=1, source_target_pairs={{0,1},{1,0},{2,3},{3,2},{4,5},{5,4},{6,7},{7,6},{8,9},{9,8},{10,11... | collective-permute-start | bytes 2359304 | tf_op jit(solution)/shard_map/ppermute | solution.py:14
  956.2 17.5 %collective-permute-start.26 = (f32[16,384]{1,0:T(8,128)S(1)}, f32[16,384]{1,0:T(8,128)S(1)}, u32[]{:S(2)}, u32[]{:S(2)}) collective-permute-start(f32[16,384]{1,0:T(8,128)S(1)} %get-tuple-element.1152), channel_id=1, source_target_pairs={{0,7},{1,8},{2,9},{3,10},{4,11},{5,12},{6,13},{7,14},{8,15},{9,16}... | collective-permute-start | bytes 73736
  957.5 24.7 %collective-permute-start.25 = (f32[16,384]{1,0:T(8,128)S(1)}, f32[16,384]{1,0:T(8,128)S(1)}, u32[]{:S(2)}, u32[]{:S(2)}) collective-permute-start(f32[16,384]{1,0:T(8,128)S(1)} %get-tuple-element.1152), channel_id=1, source_target_pairs={{0,6},{1,7},{2,8},{3,9},{4,10},{5,11},{6,12},{7,13},{8,14},{9,15},... | collective-permute-start | bytes 73736
  958.8 25.3 %collective-permute-start.24 = (f32[16,384]{1,0:T(8,128)S(1)}, f32[16,384]{1,0:T(8,128)S(1)}, u32[]{:S(2)}, u32[]{:S(2)}) collective-permute-start(f32[16,384]{1,0:T(8,128)S(1)} %get-tuple-element.1152), channel_id=1, source_target_pairs={{0,5},{1,6},{2,7},{3,8},{4,9},{5,10},{6,11},{7,12},{8,13},{9,14},{... | collective-permute-start | bytes 73736
  960.1 27.8 %collective-permute-start.23 = (f32[16,384]{1,0:T(8,128)S(1)}, f32[16,384]{1,0:T(8,128)S(1)}, u32[]{:S(2)}, u32[]{:S(2)}) collective-permute-start(f32[16,384]{1,0:T(8,128)S(1)} %get-tuple-element.1152), channel_id=1, source_target_pairs={{0,4},{1,5},{2,6},{3,7},{4,8},{5,9},{6,10},{7,11},{8,12},{9,13},{1... | collective-permute-start | bytes 73736
  961.4 10.4 collective-permute-start.27
  971.9 18.1 %collective-permute-start.22 = (f32[16,384]{1,0:T(8,128)S(1)}, f32[16,384]{1,0:T(8,128)}, u32[]{:S(2)}, u32[]{:S(2)}) collective-permute-start(f32[16,384]{1,0:T(8,128)S(1)} %get-tuple-element.1152), channel_id=1, source_target_pairs={{0,3},{1,4},{2,5},{3,6},{4,7},{5,8},{6,9},{7,10},{8,11},{9,12},{10... | collective-permute-start | bytes 73736
  973.8 18.2 %collective-permute-start.21 = (f32[16,384]{1,0:T(8,128)S(1)}, f32[16,384]{1,0:T(8,128)}, u32[]{:S(2)}, u32[]{:S(2)}) collective-permute-start(f32[16,384]{1,0:T(8,128)S(1)} %get-tuple-element.1152), channel_id=1, source_target_pairs={{0,2},{1,3},{2,4},{3,5},{4,6},{5,7},{6,8},{7,9},{8,10},{9,11},{10,... | collective-permute-start | bytes 73736
  982.2 11.6 %collective-permute-start.20 = (f32[16,384]{1,0:T(8,128)S(1)}, f32[16,384]{1,0:T(8,128)}, u32[]{:S(2)}, u32[]{:S(2)}) collective-permute-start(f32[16,384]{1,0:T(8,128)S(1)} %get-tuple-element.1152), channel_id=1, source_target_pairs={{0,1},{1,2},{2,3},{3,4},{4,5},{5,6},{6,7},{7,8},{8,9},{9,10},{10,1... | collective-permute-start | bytes 73736
  984.1 14.5 %collective-permute-start.18 = (f32[16,1152]{1,0:T(8,128)S(1)}, f32[16,1152]{1,0:T(8,128)}, u32[]{:S(2)}, u32[]{:S(2)}) collective-permute-start(f32[16,1152]{1,0:T(8,128)S(1)} %get-tuple-element.1151), channel_id=1, source_target_pairs={{0,7},{1,8},{2,9},{3,10},{4,11},{5,12},{6,13},{7,14},{8,15},{9,16}... | collective-permute-start | bytes 221192
  990.0 15.9 %collective-permute-start.17 = (f32[16,1152]{1,0:T(8,128)S(1)}, f32[16,1152]{1,0:T(8,128)}, u32[]{:S(2)}, u32[]{:S(2)}) collective-permute-start(f32[16,1152]{1,0:T(8,128)S(1)} %get-tuple-element.1151), channel_id=1, source_target_pairs={{0,6},{1,7},{2,8},{3,9},{4,10},{5,11},{6,12},{7,13},{8,14},{9,15},... | collective-permute-start | bytes 221192
  991.9 15.9 %collective-permute-start.16 = (f32[16,1152]{1,0:T(8,128)S(1)}, f32[16,1152]{1,0:T(8,128)}, u32[]{:S(2)}, u32[]{:S(2)}) collective-permute-start(f32[16,1152]{1,0:T(8,128)S(1)} %get-tuple-element.1151), channel_id=1, source_target_pairs={{0,5},{1,6},{2,7},{3,8},{4,9},{5,10},{6,11},{7,12},{8,13},{9,14},{... | collective-permute-start | bytes 221192
  993.8 15.3 %collective-permute-start.15 = (f32[16,1152]{1,0:T(8,128)S(1)}, f32[16,1152]{1,0:T(8,128)}, u32[]{:S(2)}, u32[]{:S(2)}) collective-permute-start(f32[16,1152]{1,0:T(8,128)S(1)} %get-tuple-element.1151), channel_id=1, source_target_pairs={{0,4},{1,5},{2,6},{3,7},{4,8},{5,9},{6,10},{7,11},{8,12},{9,13},{1... | collective-permute-start | bytes 221192
  995.9 15.2 %collective-permute-start.14 = (f32[16,1152]{1,0:T(8,128)S(1)}, f32[16,1152]{1,0:T(8,128)}, u32[]{:S(2)}, u32[]{:S(2)}) collective-permute-start(f32[16,1152]{1,0:T(8,128)S(1)} %get-tuple-element.1151), channel_id=1, source_target_pairs={{0,3},{1,4},{2,5},{3,6},{4,7},{5,8},{6,9},{7,10},{8,11},{9,12},{10... | collective-permute-start | bytes 221192
  998.7 12.4 %collective-permute-start.13 = (f32[16,1152]{1,0:T(8,128)S(1)}, f32[16,1152]{1,0:T(8,128)}, u32[]{:S(2)}, u32[]{:S(2)}) collective-permute-start(f32[16,1152]{1,0:T(8,128)S(1)} %get-tuple-element.1151), channel_id=1, source_target_pairs={{0,2},{1,3},{2,4},{3,5},{4,6},{5,7},{6,8},{7,9},{8,10},{9,11},{10,... | collective-permute-start | bytes 221192
  1005.9 18.4 %collective-permute-start.12 = (f32[16,1152]{1,0:T(8,128)S(1)}, f32[16,1152]{1,0:T(8,128)}, u32[]{:S(2)}, u32[]{:S(2)}) collective-permute-start(f32[16,1152]{1,0:T(8,128)S(1)} %get-tuple-element.1151), channel_id=1, source_target_pairs={{0,1},{1,2},{2,3},{3,4},{4,5},{5,6},{6,7},{7,8},{8,9},{9,10},{10,1... | collective-permute-start | bytes 221192
  1007.8 21.7 %collective-permute-start.34 = (f32[16,1536]{1,0:T(8,128)S(1)}, f32[16,1536]{1,0:T(8,128)S(1)}, u32[]{:S(2)}, u32[]{:S(2)}) collective-permute-start(f32[16,1536]{1,0:T(8,128)S(1)} %get-tuple-element.1153), channel_id=1, source_target_pairs={{0,7},{1,8},{2,9},{3,10},{4,11},{5,12},{6,13},{7,14},{8,15},{9,16}... | collective-permute-start | bytes 294920
  1009.1 17.7 %collective-permute-start.35 = (f32[12,1536]{1,0:T(8,128)}, f32[12,1536]{1,0:T(8,128)}, u32[]{:S(2)}, u32[]{:S(2)}) collective-permute-start(f32[12,1536]{1,0:T(8,128)} %slice.255), channel_id=1, source_target_pairs={{0,8},{1,9},{2,10},{3,11},{4,12},{5,13},{6,14},{7,15},{8,16},{9,17... | collective-permute-start | bytes 221192
  1011.1 60.5 %collective-permute-start.9 = (bf16[1024,384]{1,0:T(8,128)(2,1)}, bf16[1024,384]{1,0:T(8,128)(2,1)}, u32[]{:S(2)}, u32[]{:S(2)}) collective-permute-start(bf16[1024,384]{1,0:T(8,128)(2,1)} %slice.338), channel_id=1, source_target_pairs={{0,1},{1,0},{2,3},{3,2},{4,5},{5,4},{6,7},{7,6},{8,9},{9,8},{10,11... | collective-permute-start | bytes 2359304 | tf_op jit(solution)/shard_map/ppermute | solution.py:14
  1011.1 60.5 %collective-permute-start.11 = (bf16[1024,384]{1,0:T(8,128)(2,1)}, bf16[1024,384]{1,0:T(8,128)(2,1)S(1)}, u32[]{:S(2)}, u32[]{:S(2)}) collective-permute-start(bf16[1024,384]{1,0:T(8,128)(2,1)} %slice.337), channel_id=1, source_target_pairs={{0,1},{1,0},{2,3},{3,2},{4,5},{5,4},{6,7},{7,6},{8,9},{9,8},{10,11... | collective-permute-start | bytes 2359304 | tf_op jit(solution)/shard_map/ppermute | solution.py:14
  1024.3 22.9 %collective-permute-start.33 = (f32[16,1536]{1,0:T(8,128)S(1)}, f32[16,1536]{1,0:T(8,128)}, u32[]{:S(2)}, u32[]{:S(2)}) collective-permute-start(f32[16,1536]{1,0:T(8,128)S(1)} %get-tuple-element.1153), channel_id=1, source_target_pairs={{0,6},{1,7},{2,8},{3,9},{4,10},{5,11},{6,12},{7,13},{8,14},{9,15},... | collective-permute-start | bytes 294920
  1026.8 21.6 %collective-permute-start.32 = (f32[16,1536]{1,0:T(8,128)S(1)}, f32[16,1536]{1,0:T(8,128)}, u32[]{:S(2)}, u32[]{:S(2)}) collective-permute-start(f32[16,1536]{1,0:T(8,128)S(1)} %get-tuple-element.1153), channel_id=1, source_target_pairs={{0,5},{1,6},{2,7},{3,8},{4,9},{5,10},{6,11},{7,12},{8,13},{9,14},{... | collective-permute-start | bytes 294920
  1029.5 22.1 %collective-permute-start.31 = (f32[16,1536]{1,0:T(8,128)S(1)}, f32[16,1536]{1,0:T(8,128)}, u32[]{:S(2)}, u32[]{:S(2)}) collective-permute-start(f32[16,1536]{1,0:T(8,128)S(1)} %get-tuple-element.1153), channel_id=1, source_target_pairs={{0,4},{1,5},{2,6},{3,7},{4,8},{5,9},{6,10},{7,11},{8,12},{9,13},{1... | collective-permute-start | bytes 294920
  (258 other events, 2940.6 us)
Sparse Core Ops, SparseCore 0:
  10.9 57.6 all-gather.7
  248.8 51.4 all-gather.5
  636.5 98.5 reduce-scatter.7
where the time goes:
time: 1150 us; the launch traced here: 1140 us
  matrix products  301 us (26%)
  local copies, waits for them, and re-layouts  298 us (26%)
  blocking collectives  249 us (22%)
  other arithmetic  138 us (12%)
  starting transfers between devices  60.1 us (5%)
  loops' own time  43.2 us (4%)
  waiting for transfers between devices  29.1 us (3%)
  between operations  20.8 us (2%)
    unnamed x3, blocking collectives  164 us
    unnamed x486, local copies, waits for them, and re-layouts  92 us
    dynamic_update_slice x24, local copies, waits for them, and re-layouts, attend_back(): lax.scan(one_block, (empty, empty), jnp.arange(row_count // block_rows))  70.3 us
    unnamed x24, starting transfers between devices  56.9 us
    dot_general x3, matrix products, body(): jnp.dot(normed_two_low, fc1_full, preferred_element_type=jnp.float32)  49.2 us
    dot_general x12, matrix products, one_block(): jnp.einsum('hqk,qhd->khd', weights.astype(jnp.bfloat16), grad_block, pref...  44.1 us
    all_gather x1, blocking collectives, body(): lax.all_gather(shards[0], 'dp', axis=0, tiled=True)  44.1 us
    all_gather x1, blocking collectives, body(): lax.all_gather(shards[1], 'dp', axis=0, tiled=True)  40.6 us
  transfers between devices with their start and end apart: 39, of which 2 were waited for; matrix products, arithmetic and copies ran while one was open for 46% of the time, Pallas kernels for 0%

commit v1 on v0

v1 whole, which is shorter than its diff:
```python
import functools
import jax
import jax.numpy as jnp
from jax import lax
from jax.experimental import pallas as pl
from jax.experimental.pallas import tpu as pltpu

F32, BF16 = jnp.float32, jnp.bfloat16
HEADS = 6
EPS = 1e-06
FAR = -1e30
V_GAIN1, V_SHIFT1, V_QKV, V_OUT, V_GAIN2, V_SHIFT2, V_FC1, V_FC2 = range(8)
G_GAIN1, G_SHIFT1, G_QKV, G_OUT, G_GAIN2, G_SHIFT2, G_FC1, G_FC2 = range(8)


def mm(a, b):
    return jnp.dot(a, b, preferred_element_type=F32)

def mm_t(a, b):
    return lax.dot_general(a, b, (((1,), (1,)), ((), ())), preferred_element_type=F32)

def t_mm(a, b):
    return lax.dot_general(a, b, (((0,), (0,)), ((), ())), preferred_element_type=F32)


def norm_rows(v):
    width = v.shape[1]
    off = v - jnp.sum(v, axis=1, keepdims=True) * (1.0 / width)
    inv = lax.rsqrt(jnp.sum(off * off, axis=1, keepdims=True) * (1.0 / width) + EPS)
    return off * inv, inv


def norm_back(n, inv, t):
    width = n.shape[1]
    a = jnp.sum(t, axis=1, keepdims=True) * (1.0 / width)
    b = jnp.sum(t * n, axis=1, keepdims=True) * (1.0 / width)
    return inv * (t - a - n * b)


def col_sum(v):
    return jnp.sum(v, axis=0, keepdims=True)


def window(meta, m, w, group, wq, wk, rows):
    length, count = meta[m, 0], meta[m, 1]
    lo = w * (length * group)
    hi = jnp.minimum(lo + length * group, length * count)
    base = (lo // 16) * 16
    sq = pl.multiple_of(jnp.minimum(base, rows - wq), 16)
    sk = pl.multiple_of(jnp.minimum(base, rows - wk), 16)
    return lo, hi, length, sq, sk


def seg_of(start, n, lo, hi, length):
    r = start + lax.broadcasted_iota(jnp.int32, (n, 128), 0)
    inside = jnp.logical_and(r >= lo, r < hi)
    return inside, jnp.where(inside, jnp.where(r >= lo + length, 1, 0), 2)


def halves(v):
    left = lax.broadcasted_iota(jnp.int32, v.shape, 1) < 64
    zero = jnp.zeros_like(v)
    return jnp.where(left, v, zero), jnp.where(left, zero, v)


def attend_fwd(meta, m, qkv_s, o_s, inv_s, e_s, group, wq, wk, pairs, width):
    rows = qkv_s.shape[0]
    scale = 0.125 * 1.4426950408889634

    def one(w, carry):
        lo, hi, length, sq, sk = window(meta, m, w, group, wq, wk, rows)
        in_q, seg_q = seg_of(sq, wq, lo, hi, length)
        _, seg_k = seg_of(sk, wk, lo, hi, length)
        lane_q = lax.broadcasted_iota(jnp.int32, (wq, 128), 1)
        lane_k = lax.broadcasted_iota(jnp.int32, (wk, 128), 1)
        aug_q = jnp.where(jnp.logical_and(lane_q != seg_q, lane_q < 3), 1.0, 0.0).astype(BF16)
        aug_k = jnp.where(lane_k == seg_k, FAR, 0.0).astype(BF16)
        ones0 = jnp.where(lane_k < 64, 1.0, 0.0).astype(BF16)
        ones1 = jnp.where(lane_k < 64, 0.0, 1.0).astype(BF16)
        for p in range(pairs):
            c = 128 * p
            q2 = qkv_s[pl.ds(sq, wq), c : c + 128]
            k0, k1 = halves(qkv_s[pl.ds(sk, wk), width + c : width + c + 128])
            v0, v1 = halves(qkv_s[pl.ds(sk, wk), 2 * width + c : 2 * width + c + 128])
            left = jnp.concatenate([q2, aug_q], axis=1)
            right = jnp.concatenate(
                [jnp.concatenate([k0, aug_k], axis=1), jnp.concatenate([k1, aug_k], axis=1)], axis=0
            )
            s = mm_t(left, right)
            parts = []
            for h in range(2):
                sh = s[:, h * wk : (h + 1) * wk]
                top = jnp.max(sh, axis=1, keepdims=True)
                parts.append(jnp.exp2((sh - top) * scale).astype(BF16))
            e = jnp.concatenate(parts, axis=1)
            e_s[w * pairs + p] = e
            vals = jnp.concatenate(
                [jnp.concatenate([v0, ones0], axis=1), jnp.concatenate([v1, ones1], axis=1)], axis=0
            )
            both = mm(e, vals)
            inv = 1.0 / both[:, 128:]
            o = (both[:, :128] * inv).astype(BF16)
            dst = (pl.ds(sq, wq), pl.ds(c, 128))
            o_s[dst] = jnp.where(in_q, o, o_s[dst])
            inv_s[dst] = jnp.where(in_q, inv, inv_s[dst])
        return carry

    lax.fori_loop(0, (meta[m, 1] + group - 1) // group, one, 0)


def attend_bwd(meta, m, qkv_s, o_s, inv_s, e_s, go_s, gqkv_s, group, wq, wk, pairs, width):
    rows = qkv_s.shape[0]

    def one(w, carry):
        lo, hi, length, sq, sk = window(meta, m, w, group, wq, wk, rows)
        in_q, _ = seg_of(sq, wq, lo, hi, length)
        in_k, _ = seg_of(sk, wk, lo, hi, length)
        for p in range(pairs):
            c = 128 * p
            e = e_s[w * pairs + p]
            q0, q1 = halves(qkv_s[pl.ds(sq, wq), c : c + 128])
            k0, k1 = halves(qkv_s[pl.ds(sk, wk), width + c : width + c + 128])
            v0, v1 = halves(qkv_s[pl.ds(sk, wk), 2 * width + c : 2 * width + c + 128])
            dst_q = (pl.ds(sq, wq), pl.ds(c, 128))
            go = (go_s[dst_q].astype(F32) * inv_s[dst_q]).astype(BF16)
            prod0, prod1 = halves(go.astype(F32) * o_s[dst_q].astype(F32))
            d = (jnp.sum(prod0, axis=1, keepdims=True), jnp.sum(prod1, axis=1, keepdims=True))
            gp = mm_t(go, jnp.concatenate([v0, v1], axis=0))
            gs = []
            for h in range(2):
                sl = slice(h * wk, (h + 1) * wk)
                gs.append((e[:, sl].astype(F32) * (gp[:, sl] - d[h])).astype(BF16))
            gq = mm(jnp.concatenate(gs, axis=1), jnp.concatenate([k0, k1], axis=0)) * 0.125
            gk = t_mm(jnp.concatenate(gs, axis=0), jnp.concatenate([q0, q1], axis=0)) * 0.125
            gv = t_mm(
                jnp.concatenate([e[:, :wk], e[:, wk:]], axis=0), jnp.concatenate(halves(go), axis=0)
            )
            gqkv_s[dst_q] = jnp.where(in_q, gq.astype(BF16), gqkv_s[dst_q])
            dst_k = (pl.ds(sk, wk), pl.ds(width + c, 128))
            gqkv_s[dst_k] = jnp.where(in_k, gk.astype(BF16), gqkv_s[dst_k])
            dst_v = (pl.ds(sk, wk), pl.ds(2 * width + c, 128))
            gqkv_s[dst_v] = jnp.where(in_k, gv.astype(BF16), gqkv_s[dst_v])
        return carry

    lax.fori_loop(0, (meta[m, 1] + group - 1) // group, one, 0)


WIDE = (1, 352, 384)
NARROW1 = (1, 224, 256)
NARROW2 = (2, 224, 256)


def layer_kernel(
    meta, x_ref, cot_ref, wqkv, wout, w1, w2, vec,
    out_ref, ig_ref, a_qkv, a_out, a_fc1, a_fc2, a_vec,
    h1_s, qkv_s, o_s, inv_s, e1_s, e2_s, h2_s, act_s, gpre_s, gy_s, gb_s, go_s, gmix_s, gqkv_s,
    phases=("p1", "af", "mlp", "wg", "ab", "p5"), tile=512, chunk=384,
):
    m = pl.program_id(0)
    rows, width = x_ref.shape[1], x_ref.shape[2]
    hidden = w1.shape[1]
    pairs = HEADS // 2
    length, count = meta[m, 0], meta[m, 1]
    total = length * count

    @pl.when(m == 0)
    def _():
        for ref in (a_qkv, a_out, a_fc1, a_fc2, a_vec):
            ref[...] = jnp.zeros_like(ref)

    def v(i, n=width):
        return vec[i : i + 1, 0:n]

    def add_vec(i, val):
        a_vec[i : i + 1, 0 : val.shape[1]] += val

    if "p1" in phases:
        def p1(i, c):
            r = pl.ds(pl.multiple_of(i * tile, tile), tile)
            n1, _ = norm_rows(x_ref[0, r, :].astype(F32))
            h1 = (n1 * v(V_GAIN1) + v(V_SHIFT1)).astype(BF16)
            h1_s[r, :] = h1
            qkv_s[r, :] = (mm(h1, wqkv[...]) + v(V_QKV, 3 * width)).astype(BF16)
            return c
        lax.fori_loop(0, rows // tile, p1, 0)

    o_s[...] = qkv_s[:, 2 * width :]

    if "af" in phases:
        fwd = functools.partial(attend_fwd, meta, m, qkv_s, o_s, inv_s)
        @pl.when(length > 256)
        def _():
            fwd(e1_s, *WIDE, pairs, width)
        @pl.when(jnp.logical_and(length <= 256, length > 128))
        def _():
            fwd(e2_s, *NARROW1, pairs, width)
        @pl.when(length <= 128)
        def _():
            fwd(e2_s, *NARROW2, pairs, width)

    if "mlp" in phases:
        def mlp(i, c):
            r = pl.ds(pl.multiple_of(i * tile, tile), tile)
            valid = (i * tile + lax.broadcasted_iota(jnp.int32, (tile, 1), 0)) < total
            mixed = x_ref[0, r, :].astype(F32) + mm(o_s[r, :], wout[...]) + v(V_OUT)
            n2, r2 = norm_rows(mixed)
            h2 = (n2 * v(V_GAIN2) + v(V_SHIFT2)).astype(BF16)
            h2_s[r, :] = h2
            gy = jnp.where(valid, cot_ref[0, r, :].astype(F32), 0.0)
            gyl = gy.astype(BF16)
            gy_s[r, :] = gyl
            add_vec(G_FC2, col_sum(gy))
            for f in range(0, hidden, chunk):
                fs = slice(f, f + chunk)
                pre = mm(h2, w1[:, fs]) + vec[V_FC1 : V_FC1 + 1, fs]
                cdf = 0.5 * lax.erf(pre * 0.7071067811865476) + 0.5
                act_s[r, fs] = (pre * cdf).astype(BF16)
                slope = cdf + pre * (jnp.exp(pre * pre * -0.5) * 0.3989422804014327)
                gpre = (slope * mm_t(gyl, w2[fs, :])).astype(BF16)
                gpre_s[r, fs] = gpre
                a_vec[G_FC1 : G_FC1 + 1, fs] += col_sum(gpre.astype(F32))
            final = mixed + mm(act_s[r, :], w2[...]) + v(V_FC2)
            out_ref[0, r, :] = jnp.where(valid, final, 0.0).astype(BF16)
            gh2 = mm_t(gpre_s[r, :], w1[...])
            add_vec(G_GAIN2, col_sum(gh2 * n2))
            add_vec(G_SHIFT2, col_sum(gh2))
            gmix = gy + norm_back(n2, r2, gh2 * v(V_GAIN2))
            gmix_s[r, :] = gmix
            gb = gmix.astype(BF16)
            gb_s[r, :] = gb
            add_vec(G_OUT, col_sum(gb.astype(F32)))
            go_s[r, :] = mm_t(gb, wout[...]).astype(BF16)
            return c
        lax.fori_loop(0, rows // tile, mlp, 0)

    if "wg" in phases:
        a_fc1[...] += t_mm(h2_s[...], gpre_s[...])
        a_fc2[...] += t_mm(act_s[...], gy_s[...])
        a_out[...] += t_mm(o_s[...], gb_s[...])

    gqkv_s[:, : 2 * width] = jnp.zeros((rows, 2 * width), BF16)
    gqkv_s[:, 2 * width :] = go_s[...]

    if "ab" in phases:
        bwd = functools.partial(attend_bwd, meta, m, qkv_s, o_s, inv_s)
        @pl.when(length > 256)
        def _():
            bwd(e1_s, go_s, gqkv_s, *WIDE, pairs, width)
        @pl.when(jnp.logical_and(length <= 256, length > 128))
        def _():
            bwd(e2_s, go_s, gqkv_s, *NARROW1, pairs, width)
        @pl.when(length <= 128)
        def _():
            bwd(e2_s, go_s, gqkv_s, *NARROW2, pairs, width)

    if "p5" in phases:
        def p5(i, c):
            r = pl.ds(pl.multiple_of(i * tile, tile), tile)
            gqkv = gqkv_s[r, :]
            gh1 = mm_t(gqkv, wqkv[...])
            n1, r1 = norm_rows(x_ref[0, r, :].astype(F32))
            add_vec(G_QKV, col_sum(gqkv.astype(F32)))
            add_vec(G_GAIN1, col_sum(gh1 * n1))
            add_vec(G_SHIFT1, col_sum(gh1))
            ig_ref[0, r, :] = (gmix_s[r, :] + norm_back(n1, r1, gh1 * v(V_GAIN1))).astype(BF16)
            return c
        lax.fori_loop(0, rows // tile, p5, 0)
        a_qkv[...] += t_mm(h1_s[...], gqkv_s[...])


def layer_call(meta, x, cot, wqkv, wout, w1, w2, vec, **kw):
    micro, rows, width = x.shape
    hidden = w1.shape[1]
    row_block = pl.BlockSpec((1, rows, width), lambda m: (m, 0, 0))
    def whole(a):
        return pl.BlockSpec(a.shape, lambda m: (0, 0), pipeline_mode=pl.Buffered(1))
    def kept(shape):
        return pl.BlockSpec(shape, lambda m: (0, 0), pipeline_mode=pl.Buffered(1))
    grads = [wqkv.shape, wout.shape, w1.shape, w2.shape, vec.shape]
    bf = lambda n: pltpu.VMEM((rows, n), BF16)
    return pl.pallas_call(
        functools.partial(layer_kernel, **kw),
        grid=(micro,),
        in_specs=[pl.BlockSpec(memory_space=pltpu.SMEM), row_block, row_block]
        + [whole(a) for a in (wqkv, wout, w1, w2, vec)],
        out_specs=[row_block, row_block] + [kept(s) for s in grads],
        out_shape=[jax.ShapeDtypeStruct(x.shape, BF16)] * 2 + [jax.ShapeDtypeStruct(s, F32) for s in grads],
        scratch_shapes=[
            bf(width), bf(3 * width), bf(width), pltpu.VMEM((rows, width), F32),
            pltpu.VMEM((9, 352, 768), BF16), pltpu.VMEM((15, 224, 512), BF16),
            bf(width), bf(hidden), bf(hidden), bf(width), bf(width), bf(width),
            pltpu.VMEM((rows, width), F32), bf(3 * width),
        ],
        compiler_params=pltpu.CompilerParams(vmem_limit_bytes=63 * 2**20),
    )(meta, x, cot, wqkv, wout, w1, w2, vec)


def body(inputs, cotangent, w_qkv, w_out, w_fc1, w_fc2, gain1, shift1, q_bias, v_bias, out_bias, gain2, shift2,
         fc1_bias, fc2_bias, image_tokens, image_count):
    j = lax.axis_index("dp")
    n = lax.axis_size("dp")
    width = w_qkv.shape[1] // 3
    hidden = w_fc1.shape[1]
    gather = functools.partial(lax.all_gather, axis_name="dp", axis=0, tiled=True)
    mats = [gather(w) for w in (w_qkv, w_out, w_fc1, w_fc2)]
    small = (gain1, shift1, q_bias, v_bias, out_bias, gain2, shift2, fc2_bias)
    packed = jnp.concatenate([jnp.stack(small).reshape(-1), fc1_bias])[None]
    packed = gather(packed).astype(F32)
    part = width // n
    cols = [packed[:, i * part : (i + 1) * part].reshape(-1) for i in range(8)]
    fc1_full = packed[:, 8 * part :].reshape(-1)
    pad = lambda a: jnp.pad(a, (0, hidden - a.shape[0]))
    qkv_bias = jnp.concatenate([cols[2], jnp.zeros_like(cols[2]), cols[3]])
    vec = jnp.stack([pad(cols[0]), pad(cols[1]), pad(qkv_bias), pad(cols[4]), pad(cols[5]), pad(cols[6]), fc1_full, pad(cols[7])])
    meta = jnp.stack([image_tokens[:, j], image_count[:, j]], axis=1)
    out, ig, g_qkv, g_out, g_fc1, g_fc2, g_vec = layer_call(meta, inputs, cotangent, *mats, vec)
    scatter = functools.partial(lax.psum_scatter, axis_name="dp", scatter_dimension=0, tiled=True)
    grads = [scatter(g) for g in (g_qkv, g_out, g_fc1, g_fc2)]
    own = [g_vec[0, :width], g_vec[1, :width], g_vec[2, :width], g_vec[2, 2 * width : 3 * width], g_vec[3, :width],
           g_vec[4, :width], g_vec[5, :width], g_vec[7, :width]]
    rows = jnp.concatenate([o.reshape(n, part) for o in own] + [g_vec[6].reshape(n, -1)], axis=1)
    mine = scatter(rows)[0]
    vs = [mine[i * part : (i + 1) * part] for i in range(8)]
    return (out, ig, *grads, vs[0], vs[1], vs[2], vs[3], vs[4], vs[5], vs[6], mine[8 * part :], vs[7])


def solution(mesh):
    from jax.sharding import PartitionSpec as P
    big, mat, one = P(None, "dp", None), P("dp", None), P("dp")
    return jax.shard_map(
        body, mesh=mesh,
        in_specs=(big, big) + (mat,) * 4 + (one,) * 9 + (P(), P()),
        out_specs=(big, big) + (mat,) * 4 + (one,) * 9,
        check_vma=False,
    )
```

time: 1150 us -> 440 us (0.38)
  matrix products: 301 us -> 0 us
  local copies, waits for them, and re-layouts: 298 us -> 19 us
  other arithmetic: 138 us -> 1.4 us
  Pallas kernels: 0 us -> 89.5 us
  loops' own time: 43.2 us -> 0 us
  waiting for transfers between devices: 29.1 us -> 2.99 us
    dot_general x120 -> x0, matrix products: 301 us -> none  [the longest x3 49.2 us: body(): jnp.dot(normed_two_low, fc1_full, preferred_element_type=jnp.float32)]
    pallas_call x0 -> x1, Pallas kernels: none -> 89.5 us  [layer_call(): pl.pallas_call(functools.partial(layer_kernel, **kw), grid=(micro,), in_s...]
    unnamed x486 -> x22, local copies, waits for them, and re-layouts: 92 us -> 12.1 us
    dynamic_update_slice x27 -> x0, local copies, waits for them, and re-layouts: 70.9 us -> none  [the longest x24 70.3 us: attend_back(): lax.scan(one_block, (empty, empty), jnp.arange(row_count // block_rows))]
    reduce_sum x31 -> x0, other arithmetic: 56.8 us -> none  [the longest x12 21.6 us: one_block(): totals = jnp.sum(raised, axis=-1, keepdims=True)]
    another operation x12 -> x0, loops' own time: 43.2 us -> none  [the longest x6 34.2 us: attend_back(): lax.scan(one_block, (empty, empty), jnp.arange(row_count // block_rows))]
    convert_element_type x24 -> x0, other arithmetic: 28.1 us -> none  [the longest x12 21.8 us: one_block(): grad_scores = (weights * (grad_weights - inner)).astype(jnp.bfloat16)]
    all_gather x2, waiting for transfers between devices: 26.1 us -> 0.01 us  [body(): mats = [gather(w) for w in (w_qkv, w_out, w_fc1, w_fc2)]]
  transfers between devices with their start and end apart: 39 -> 27, of which waited for: 2 -> 1; matrix products, arithmetic and copies ran while one was open for 46% -> 24% of each run, Pallas kernels for 0% -> 0%
where the time goes in v1:
time: 440 us; the launch traced here: 438 us
  blocking collectives  249 us (57%)
  Pallas kernels  89.5 us (20%)
  starting transfers between devices  61.7 us (14%)
  local copies, waits for them, and re-layouts  19 us (4%)
  between operations  14.4 us (3%)
    unnamed x3, blocking collectives  167 us
    pallas_call x1, Pallas kernels, layer_call(): pl.pallas_call(functools.partial(layer_kernel, **kw), grid=(micro,), in_s...  89.5 us
    all_gather x2, blocking collectives, body(): mats = [gather(w) for w in (w_qkv, w_out, w_fc1, w_fc2)]  82.4 us
    unnamed x24, starting transfers between devices  61.6 us
    unnamed x22, local copies, waits for them, and re-layouts  12.1 us
  transfers between devices with their start and end apart: 27, of which 1 were waited for; matrix products, arithmetic and copies ran while one was open for 24% of the time, Pallas kernels for 0%

profile of v1, /device:TPU:0, one launch (start us, length us, event | category | flops | bytes accessed | tf_op | source)
XLA Modules:
  0.0 438.3 jit_solution(9377977995844759149)
XLA Ops:
  10.6 42.2 %all-reduce.7 = bf16[4608]{0:T(1024)(128)(2,1)S(1)} all-reduce(bf16[4608]{0:T(1024)(128)(2,1)S(1)} %dynamic-update-slice), channel_id=2, replica_groups=mesh['dp'=32] {'dp'}, use_global_device_ids=true, to_apply=%add.7 | all-reduce | flops 4608 | bytes 18432
  54.1 44.6 %all-gather.1 = bf16[32,12,1152]{2,1,0:T(8,128)(2,1)S(1)} all-gather(bf16[1,12,1152]{2,1,0:T(8,128)(2,1)} %bitcast.30), channel_id=1, replica_groups=mesh['dp'=32] {'dp'}, dimensions={0}, use_global_device_ids=true | all-gather | bytes 912384 | tf_op jit(solution)/shard_map/all_gather | solution.py:305
  100.0 37.8 %all-gather.2 = bf16[32,12,384]{2,1,0:T(8,128)(2,1)S(1)} all-gather(bf16[1,12,384]{2,1,0:T(8,128)(2,1)S(1)} %bitcast.31), channel_id=1, replica_groups=mesh['dp'=32] {'dp'}, dimensions={0}, use_global_device_ids=true | all-gather | bytes 304128 | tf_op jit(solution)/shard_map/all_gather | solution.py:305
  140.0 3.0 reshape.84.w1
  143.0 89.5 %shard_map.280 = (bf16[3,1024,384]{2,1,0:T(8,128)(2,1)}, bf16[3,1024,384]{2,1,0:T(8,128)(2,1)}, f32[384,1152]{1,0:T(8,128)}, f32[384,384]{1,0:T(8,128)}, f32[384...) custom-call(s32[3,2]{1,0:T(4,128)} %pad_add_fusion.meta, bf16[3,1024,384]{2,1,0:T(8,128)(2,1)} %x_ref.1, ...), custom_call_target="tpu_custom_call" | custom-call | tf_op jit(solution)/shard_map/pallas_call | solution.py:281
  232.6 1.6 copy-done
  234.2 86.7 %fusion.3 = (f32[16,1152]{1,0:T(8,128)S(1)}, f32[16,384]{1,0:T(8,128)S(1)}, f32[16,1536]{1,0:T(8,128)S(1)}) fusion(f32[384,1152]{1,0:T(8,128)} %get-tuple-element.24, f32[384,384]{1,0:T(8,128)} %get-tuple-element.25, f32[384,1536]{1,0:T(8,128)S(1)} %copy-done), kind=kCustom, calls=%all-reduce-scatter.3 | all-reduce-scatter fusion | flops 1572865 | bytes 4915200
  321.0 1.3 collective-permute-start.10
  322.3 1.3 collective-permute-start.11
  323.6 3.2 collective-permute-start.12
  329.9 4.6 %collective-permute-start.13 = (f32[16,384]{1,0:T(8,128)S(1)}, f32[16,384]{1,0:T(8,128)S(1)}, u32[]{:S(2)}, u32[]{:S(2)}) collective-permute-start(f32[16,384]{1,0:T(8,128)S(1)} %get-tuple-element.41), channel_id=1, source_target_pairs={{0,6},{1,7},{2,8},{3,9},{4,10},{5,11},{6,12},{7,13},{8,14},{9,15},... | collective-permute-start | bytes 73736
  335.6 37.9 %all-reduce.11 = f32[32,144]{1,0:T(8,128)S(1)} all-reduce(f32[32,144]{1,0:T(8,128)S(1)} %concatenate.11), channel_id=7, replica_groups=mesh['dp'=32] {'dp'}, use_global_device_ids=true, to_apply=%region_4.5.clone | all-reduce | flops 4608 | bytes 36864
  373.5 2.9 collective-permute-start.14
  376.4 3.1 collective-permute-start.8
  379.5 4.1 collective-permute-start.9
  383.7 2.6 collective-permute-start.7
  386.9 2.2 collective-permute-start
  389.1 3.1 collective-permute-start.1
  392.2 2.8 collective-permute-start.2
  395.1 3.3 collective-permute-start.3
  398.5 1.6 collective-permute-start.4
  401.6 3.2 collective-permute-start.16
  404.8 2.5 collective-permute-start.17
  407.3 3.2 collective-permute-start.5
  410.6 1.8 collective-permute-start.6
  412.4 1.3 collective-permute-start.23
  414.3 1.4 collective-permute-start.18
  415.7 3.7 collective-permute-start.19
  420.5 2.7 collective-permute-start.20
  423.3 2.9 collective-permute-start.21
  426.1 1.5 collective-permute-start.22
  428.3 1.5 collective-permute-done.22
  (100 shorter events, 18.7 us)
Async XLA Ops:
  7.2 92.8 %copy-start.1 = (bf16[12,384]{1,0:T(8,128)(2,1)S(1)}, bf16[12,384]{1,0:T(8,128)(2,1)}, u32[]{:S(2)}) copy-start(bf16[12,384]{1,0:T(8,128)(2,1)} %param.20) | copy-start | bytes 27652
  7.2 132.8 %all-gather.9.cloned.1.call-start = ((), (), s32[]{:S(2)}) async-start(), calls=%async_computation.3 | async-start | bytes 1622016 | tf_op jit(solution)/shard_map/all_gather | solution.py:305
  7.9 135.1 %all-gather.7.cloned.1.call-start = ((), (), s32[]{:S(2)}) async-start(), calls=%async_computation.1 | async-start | bytes 1216512 | tf_op jit(solution)/shard_map/all_gather | solution.py:305
  8.7 423.1 %reduce-scatter.8.cloned.1.call-start = ((), (), s32[]{:S(2)}) async-start(), calls=%async_computation.2 | async-start | bytes 2433024 | tf_op jit(solution)/shard_map/reduce_scatter | solution.py:318
  53.5 85.8 %copy-start.2 = (s32[3,32]{1,0:T(4,128)S(1)}, s32[3,32]{1,0:T(4,128)}, u32[]{:S(2)}) copy-start(s32[3,32]{1,0:T(4,128)} %param.33) | copy-start | bytes 1156
  53.5 85.8 %copy-start.3 = (s32[3,32]{1,0:T(4,128)S(1)}, s32[3,32]{1,0:T(4,128)}, u32[]{:S(2)}) copy-start(s32[3,32]{1,0:T(4,128)} %param.32) | copy-start | bytes 1156
  232.6 1.7 copy-start
  321.0 55.4 %collective-permute-start.10 = (f32[16,384]{1,0:T(8,128)S(1)}, f32[16,384]{1,0:T(8,128)S(1)}, u32[]{:S(2)}, u32[]{:S(2)}) collective-permute-start(f32[16,384]{1,0:T(8,128)S(1)} %get-tuple-element.41), channel_id=1, source_target_pairs={{0,3},{1,4},{2,5},{3,6},{4,7},{5,8},{6,9},{7,10},{8,11},{9,12},{10... | collective-permute-start | bytes 73736
  322.3 57.2 %collective-permute-start.11 = (f32[16,384]{1,0:T(8,128)S(1)}, f32[16,384]{1,0:T(8,128)S(1)}, u32[]{:S(2)}, u32[]{:S(2)}) collective-permute-start(f32[16,384]{1,0:T(8,128)S(1)} %get-tuple-element.41), channel_id=1, source_target_pairs={{0,4},{1,5},{2,6},{3,7},{4,8},{5,9},{6,10},{7,11},{8,12},{9,13},{1... | collective-permute-start | bytes 73736
  323.6 60.1 %collective-permute-start.12 = (f32[16,384]{1,0:T(8,128)S(1)}, f32[16,384]{1,0:T(8,128)S(1)}, u32[]{:S(2)}, u32[]{:S(2)}) collective-permute-start(f32[16,384]{1,0:T(8,128)S(1)} %get-tuple-element.41), channel_id=1, source_target_pairs={{0,5},{1,6},{2,7},{3,8},{4,9},{5,10},{6,11},{7,12},{8,13},{9,14},{... | collective-permute-start | bytes 73736
  326.8 46.7 %collective-permute-start.15 = (f32[12,384]{1,0:T(8,128)S(1)}, f32[12,384]{1,0:T(8,128)S(1)}, u32[]{:S(2)}, u32[]{:S(2)}) collective-permute-start(f32[12,384]{1,0:T(8,128)S(1)} %slice.154), channel_id=1, source_target_pairs={{0,8},{1,9},{2,10},{3,11},{4,12},{5,13},{6,14},{7,15},{8,16},{9,17... | collective-permute-start | bytes 55304
  329.9 57.0 %collective-permute-start.13 = (f32[16,384]{1,0:T(8,128)S(1)}, f32[16,384]{1,0:T(8,128)S(1)}, u32[]{:S(2)}, u32[]{:S(2)}) collective-permute-start(f32[16,384]{1,0:T(8,128)S(1)} %get-tuple-element.41), channel_id=1, source_target_pairs={{0,6},{1,7},{2,8},{3,9},{4,10},{5,11},{6,12},{7,13},{8,14},{9,15},... | collective-permute-start | bytes 73736
  373.5 15.6 %collective-permute-start.14 = (f32[16,384]{1,0:T(8,128)S(1)}, f32[16,384]{1,0:T(8,128)S(1)}, u32[]{:S(2)}, u32[]{:S(2)}) collective-permute-start(f32[16,384]{1,0:T(8,128)S(1)} %get-tuple-element.41), channel_id=1, source_target_pairs={{0,7},{1,8},{2,9},{3,10},{4,11},{5,12},{6,13},{7,14},{8,15},{9,16}... | collective-permute-start | bytes 73736
  376.4 15.9 %collective-permute-start.8 = (f32[16,384]{1,0:T(8,128)S(1)}, f32[16,384]{1,0:T(8,128)S(1)}, u32[]{:S(2)}, u32[]{:S(2)}) collective-permute-start(f32[16,384]{1,0:T(8,128)S(1)} %get-tuple-element.41), channel_id=1, source_target_pairs={{0,1},{1,2},{2,3},{3,4},{4,5},{5,6},{6,7},{7,8},{8,9},{9,10},{10,1... | collective-permute-start | bytes 73736
  379.5 15.6 %collective-permute-start.9 = (f32[16,384]{1,0:T(8,128)S(1)}, f32[16,384]{1,0:T(8,128)S(1)}, u32[]{:S(2)}, u32[]{:S(2)}) collective-permute-start(f32[16,384]{1,0:T(8,128)S(1)} %get-tuple-element.41), channel_id=1, source_target_pairs={{0,2},{1,3},{2,4},{3,5},{4,6},{5,7},{6,8},{7,9},{8,10},{9,11},{10,... | collective-permute-start | bytes 73736
  383.7 14.8 %collective-permute-start.7 = (f32[12,1152]{1,0:T(8,128)S(1)}, f32[12,1152]{1,0:T(8,128)S(1)}, u32[]{:S(2)}, u32[]{:S(2)}) collective-permute-start(f32[12,1152]{1,0:T(8,128)S(1)} %slice.153), channel_id=1, source_target_pairs={{0,8},{1,9},{2,10},{3,11},{4,12},{5,13},{6,14},{7,15},{8,16},{9,17... | collective-permute-start | bytes 165896
  386.9 14.7 %collective-permute-start = (f32[16,1152]{1,0:T(8,128)S(1)}, f32[16,1152]{1,0:T(8,128)S(1)}, u32[]{:S(2)}, u32[]{:S(2)}) collective-permute-start(f32[16,1152]{1,0:T(8,128)S(1)} %get-tuple-element.40), channel_id=1, source_target_pairs={{0,1},{1,2},{2,3},{3,4},{4,5},{5,6},{6,7},{7,8},{8,9},{9,10},{10,1... | collective-permute-start | bytes 221192
  389.1 15.7 %collective-permute-start.1 = (f32[16,1152]{1,0:T(8,128)S(1)}, f32[16,1152]{1,0:T(8,128)S(1)}, u32[]{:S(2)}, u32[]{:S(2)}) collective-permute-start(f32[16,1152]{1,0:T(8,128)S(1)} %get-tuple-element.40), channel_id=1, source_target_pairs={{0,2},{1,3},{2,4},{3,5},{4,6},{5,7},{6,8},{7,9},{8,10},{9,11},{10,... | collective-permute-start | bytes 221192
  392.2 15.1 %collective-permute-start.2 = (f32[16,1152]{1,0:T(8,128)S(1)}, f32[16,1152]{1,0:T(8,128)S(1)}, u32[]{:S(2)}, u32[]{:S(2)}) collective-permute-start(f32[16,1152]{1,0:T(8,128)S(1)} %get-tuple-element.40), channel_id=1, source_target_pairs={{0,3},{1,4},{2,5},{3,6},{4,7},{5,8},{6,9},{7,10},{8,11},{9,12},{10... | collective-permute-start | bytes 221192
  395.1 15.4 %collective-permute-start.3 = (f32[16,1152]{1,0:T(8,128)S(1)}, f32[16,1152]{1,0:T(8,128)S(1)}, u32[]{:S(2)}, u32[]{:S(2)}) collective-permute-start(f32[16,1152]{1,0:T(8,128)S(1)} %get-tuple-element.40), channel_id=1, source_target_pairs={{0,4},{1,5},{2,6},{3,7},{4,8},{5,9},{6,10},{7,11},{8,12},{9,13},{1... | collective-permute-start | bytes 221192
  398.5 13.9 %collective-permute-start.4 = (f32[16,1152]{1,0:T(8,128)S(1)}, f32[16,1152]{1,0:T(8,128)S(1)}, u32[]{:S(2)}, u32[]{:S(2)}) collective-permute-start(f32[16,1152]{1,0:T(8,128)S(1)} %get-tuple-element.40), channel_id=1, source_target_pairs={{0,5},{1,6},{2,7},{3,8},{4,9},{5,10},{6,11},{7,12},{8,13},{9,14},{... | collective-permute-start | bytes 221192
  401.6 21.6 %collective-permute-start.16 = (f32[16,1536]{1,0:T(8,128)S(1)}, f32[16,1536]{1,0:T(8,128)S(1)}, u32[]{:S(2)}, u32[]{:S(2)}) collective-permute-start(f32[16,1536]{1,0:T(8,128)S(1)} %get-tuple-element.42), channel_id=1, source_target_pairs={{0,1},{1,2},{2,3},{3,4},{4,5},{5,6},{6,7},{7,8},{8,9},{9,10},{10,1... | collective-permute-start | bytes 294920
  404.8 21.3 %collective-permute-start.17 = (f32[16,1536]{1,0:T(8,128)S(1)}, f32[16,1536]{1,0:T(8,128)S(1)}, u32[]{:S(2)}, u32[]{:S(2)}) collective-permute-start(f32[16,1536]{1,0:T(8,128)S(1)} %get-tuple-element.42), channel_id=1, source_target_pairs={{0,2},{1,3},{2,4},{3,5},{4,6},{5,7},{6,8},{7,9},{8,10},{9,11},{10,... | collective-permute-start | bytes 294920
  407.3 7.0 %collective-permute-start.5 = (f32[16,1152]{1,0:T(8,128)S(1)}, f32[16,1152]{1,0:T(8,128)S(1)}, u32[]{:S(2)}, u32[]{:S(2)}) collective-permute-start(f32[16,1152]{1,0:T(8,128)S(1)} %get-tuple-element.40), channel_id=1, source_target_pairs={{0,6},{1,7},{2,8},{3,9},{4,10},{5,11},{6,12},{7,13},{8,14},{9,15},... | collective-permute-start | bytes 221192
  410.6 5.1 %collective-permute-start.6 = (f32[16,1152]{1,0:T(8,128)S(1)}, f32[16,1152]{1,0:T(8,128)S(1)}, u32[]{:S(2)}, u32[]{:S(2)}) collective-permute-start(f32[16,1152]{1,0:T(8,128)S(1)} %get-tuple-element.40), channel_id=1, source_target_pairs={{0,7},{1,8},{2,9},{3,10},{4,11},{5,12},{6,13},{7,14},{8,15},{9,16}... | collective-permute-start | bytes 221192
  412.4 8.1 %collective-permute-start.23 = (f32[12,1536]{1,0:T(8,128)S(1)}, f32[12,1536]{1,0:T(8,128)S(1)}, u32[]{:S(2)}, u32[]{:S(2)}) collective-permute-start(f32[12,1536]{1,0:T(8,128)S(1)} %slice.155), channel_id=1, source_target_pairs={{0,8},{1,9},{2,10},{3,11},{4,12},{5,13},{6,14},{7,15},{8,16},{9,17... | collective-permute-start | bytes 221192
  414.3 14.0 %collective-permute-start.18 = (f32[16,1536]{1,0:T(8,128)S(1)}, f32[16,1536]{1,0:T(8,128)S(1)}, u32[]{:S(2)}, u32[]{:S(2)}) collective-permute-start(f32[16,1536]{1,0:T(8,128)S(1)} %get-tuple-element.42), channel_id=1, source_target_pairs={{0,3},{1,4},{2,5},{3,6},{4,7},{5,8},{6,9},{7,10},{8,11},{9,12},{10... | collective-permute-start | bytes 294920
  415.7 12.6 %collective-permute-start.19 = (f32[16,1536]{1,0:T(8,128)S(1)}, f32[16,1536]{1,0:T(8,128)S(1)}, u32[]{:S(2)}, u32[]{:S(2)}) collective-permute-start(f32[16,1536]{1,0:T(8,128)S(1)} %get-tuple-element.42), channel_id=1, source_target_pairs={{0,4},{1,5},{2,6},{3,7},{4,8},{5,9},{6,10},{7,11},{8,12},{9,13},{1... | collective-permute-start | bytes 294920
  420.5 7.8 %collective-permute-start.20 = (f32[16,1536]{1,0:T(8,128)S(1)}, f32[16,1536]{1,0:T(8,128)S(1)}, u32[]{:S(2)}, u32[]{:S(2)}) collective-permute-start(f32[16,1536]{1,0:T(8,128)S(1)} %get-tuple-element.42), channel_id=1, source_target_pairs={{0,5},{1,6},{2,7},{3,8},{4,9},{5,10},{6,11},{7,12},{8,13},{9,14},{... | collective-permute-start | bytes 294920
  423.3 5.1 %collective-permute-start.21 = (f32[16,1536]{1,0:T(8,128)S(1)}, f32[16,1536]{1,0:T(8,128)S(1)}, u32[]{:S(2)}, u32[]{:S(2)}) collective-permute-start(f32[16,1536]{1,0:T(8,128)S(1)} %get-tuple-element.42), channel_id=1, source_target_pairs={{0,6},{1,7},{2,8},{3,9},{4,10},{5,11},{6,12},{7,13},{8,14},{9,15},... | collective-permute-start | bytes 294920
  426.1 3.7 collective-permute-start.22
Sparse Core Ops, SparseCore 0:
  10.9 58.4 all-gather.8
  72.3 54.1 all-gather.6
  232.7 109.6 reduce-scatter.7

commit v2 on v1

--- a/solution.py
+++ b/solution.py
@@ -1,11 +1,15 @@
 import functools
+
 import jax
 import jax.numpy as jnp
 from jax import lax
 from jax.experimental import pallas as pl
 from jax.experimental.pallas import tpu as pltpu
+from jax.sharding import PartitionSpec as P
 
 F32, BF16 = jnp.float32, jnp.bfloat16
+MESH = pl.DeviceIdType.MESH
+
 HEADS = 6
 EPS = 1e-06
 FAR = -1e30
@@ -150,10 +154,79 @@
 NARROW2 = (2, 224, 256)
 
 
+def fold_matrix(part, count, high):
+    rows, cols = 4 * count * part, count * high
+    r = lax.broadcasted_iota(jnp.int32, (rows, cols), 0).astype(F32)
+    c = lax.broadcasted_iota(jnp.int32, (rows, cols), 1).astype(F32)
+    block = jnp.floor((c + 0.5) * (1.0 / high))
+    inner = c - block * high
+    piece = jnp.floor((inner + 0.5) * (1.0 / part))
+    want = piece * (count * part) + block * part + (inner - piece * part)
+    return jnp.where(jnp.logical_and(want == r, piece < 4), 1.0, 0.0).astype(BF16)
+
+
+def unfold(src, dsts, part):
+    width = dsts[0].shape[0]
+    n = width // part
+    high = src.shape[0] // n
+    count = 96 // part
+    pick = fold_matrix(part, count, high)
+    for t in range(n // count):
+        full = mm(pick, src[t * count * high : (t + 1) * count * high, :]).astype(BF16)
+        for a in range(4):
+            dsts[a][96 * t : 96 * (t + 1), :] = full[96 * a : 96 * (a + 1), :]
+
+
+def fold(srcs, dst, part):
+    width = srcs[0].shape[0]
+    n = width // part
+    high = dst.shape[0] // n
+    count = 96 // part
+    pick = fold_matrix(part, count, high)
+    for t in range(n // count):
+        rows = slice(96 * t, 96 * (t + 1))
+        four = jnp.concatenate([s[rows, :].astype(BF16) for s in srcs], axis=0)
+        dst[t * count * high : (t + 1) * count * high, :] = t_mm(pick, four).astype(BF16)
+
+
+def unfold_vectors(src, vec, part):
+    n = src.shape[0]
+    width = part * n
+    lane = lax.broadcasted_iota(jnp.int32, (8, 128), 1)
+    total = jnp.zeros((8, width), F32)
+    wide = jnp.zeros((8, 4 * width), F32)
+    for j in range(n):
+        one = jnp.where(lane < part, src[j, 0:8, :], 0.0)
+        one = jnp.concatenate([one, jnp.zeros((8, width - 128), F32)], axis=1)
+        total = total + pltpu.roll(one, j * part, 1)
+        one = jnp.where(lane < 4 * part, src[j, 8:16, :], 0.0)
+        one = jnp.concatenate([one, jnp.zeros((8, 4 * width - 128), F32)], axis=1)
+        wide = wide + pltpu.roll(one, 4 * j * part, 1)
+    vec[...] = jnp.zeros_like(vec)
+    for i, (row, col) in enumerate(VECTORS):
+        vec[row : row + 1, col * width : (col + 1) * width] = total[i : i + 1]
+    vec[V_FC1 : V_FC1 + 1, :] = wide[0:1]
+
+
+def fold_vectors(vec, dst, part):
+    n = dst.shape[0]
+    width = part * n
+    eight = jnp.concatenate(
+        [vec[row : row + 1, col * width : (col + 1) * width] for row, col in VECTORS], axis=0
+    )
+    wide = jnp.broadcast_to(vec[V_FC1 : V_FC1 + 1, :], (8, 4 * width))
+    for j in range(n):
+        dst[j, 0:8, :] = pltpu.roll(eight, (width - j * part) % width, 1)[:, :128]
+        dst[j, 8:16, :] = pltpu.roll(wide, (4 * width - 4 * j * part) % (4 * width), 1)[:, :128]
+
+
+VECTORS = ((V_GAIN1, 0), (V_SHIFT1, 0), (V_QKV, 0), (V_QKV, 2), (V_OUT, 0), (V_GAIN2, 0), (V_SHIFT2, 0), (V_FC2, 0))
+
+
 def layer_kernel(
-    meta, x_ref, cot_ref, wqkv, wout, w1, w2, vec,
-    out_ref, ig_ref, a_qkv, a_out, a_fc1, a_fc2, a_vec,
-    h1_s, qkv_s, o_s, inv_s, e1_s, e2_s, h2_s, act_s, gpre_s, gy_s, gb_s, go_s, gmix_s, gqkv_s,
+    meta, x_ref, cot_ref, g_attn, g_fc1, w2, g_vec,
+    out_ref, ig_ref, p_attn, p_fc1, p_fc2, p_vec,
+    wqkv, wout, w1, vec, a_qkv, a_out, a_fc1, a_fc2, a_vec, h1_s, qkv_s, o_s, inv_s, e1_s, e2_s, h2_s, act_s, gpre_s, gy_s, gb_s, go_s, gmix_s, gqkv_s,
     phases=("p1", "af", "mlp", "wg", "ab", "p5"), tile=512, chunk=384,
 ):
     m = pl.program_id(0)
@@ -162,9 +235,13 @@
     pairs = HEADS // 2
     length, count = meta[m, 0], meta[m, 1]
     total = length * count
+    part = width // g_vec.shape[0]
 
     @pl.when(m == 0)
     def _():
+        unfold(g_attn, [wqkv.at[:, 0:width], wqkv.at[:, width : 2 * width], wqkv.at[:, 2 * width :], wout], part)
+        unfold(g_fc1, [w1.at[:, i * width : (i + 1) * width] for i in range(4)], part)
+        unfold_vectors(g_vec, vec, part)
         for ref in (a_qkv, a_out, a_fc1, a_fc2, a_vec):
             ref[...] = jnp.zeros_like(ref)
 
@@ -267,65 +344,213 @@
         lax.fori_loop(0, rows // tile, p5, 0)
         a_qkv[...] += t_mm(h1_s[...], gqkv_s[...])
 
-
-def layer_call(meta, x, cot, wqkv, wout, w1, w2, vec, **kw):
+    @pl.when(m == pl.num_programs(0) - 1)
+    def _():
+        fold([a_qkv.at[:, 0:width], a_qkv.at[:, width : 2 * width], a_qkv.at[:, 2 * width :], a_out], p_attn, part)
+        fold([a_fc1.at[:, i * width : (i + 1) * width] for i in range(4)], p_fc1, part)
+        p_fc2[...] = a_fc2[...].astype(BF16)
+        fold_vectors(a_vec, p_vec, part)
+
+
+def layer_call(meta, x, cot, g_attn, g_fc1, w2, g_vec, **kw):
     micro, rows, width = x.shape
-    hidden = w1.shape[1]
+    hidden = w2.shape[0]
     row_block = pl.BlockSpec((1, rows, width), lambda m: (m, 0, 0))
     def whole(a):
-        return pl.BlockSpec(a.shape, lambda m: (0, 0), pipeline_mode=pl.Buffered(1))
-    def kept(shape):
-        return pl.BlockSpec(shape, lambda m: (0, 0), pipeline_mode=pl.Buffered(1))
-    grads = [wqkv.shape, wout.shape, w1.shape, w2.shape, vec.shape]
+        zeros = (0,) * len(a.shape)
+        return pl.BlockSpec(a.shape, lambda m: zeros, pipeline_mode=pl.Buffered(1))
+    gathered = (g_attn, g_fc1, w2, g_vec)
     bf = lambda n: pltpu.VMEM((rows, n), BF16)
+    w_shapes = [(width, 3 * width), (width, width), (width, hidden), (hidden, width)]
     return pl.pallas_call(
         functools.partial(layer_kernel, **kw),
         grid=(micro,),
-        in_specs=[pl.BlockSpec(memory_space=pltpu.SMEM), row_block, row_block]
-        + [whole(a) for a in (wqkv, wout, w1, w2, vec)],
-        out_specs=[row_block, row_block] + [kept(s) for s in grads],
-        out_shape=[jax.ShapeDtypeStruct(x.shape, BF16)] * 2 + [jax.ShapeDtypeStruct(s, F32) for s in grads],
-        scratch_shapes=[
+        in_specs=[pl.BlockSpec(memory_space=pltpu.SMEM), row_block, row_block] + [whole(a) for a in gathered],
+        out_specs=[row_block, row_block] + [whole(a) for a in gathered],
+        out_shape=[jax.ShapeDtypeStruct(x.shape, BF16)] * 2 + [jax.ShapeDtypeStruct(a.shape, a.dtype) for a in gathered],
+        scratch_shapes=[pltpu.VMEM(s, BF16) for s in w_shapes[:3]] + [pltpu.VMEM((8, hidden), F32)]
+        + [pltpu.VMEM(s, F32) for s in w_shapes] + [pltpu.VMEM((8, hidden), F32)] + [
             bf(width), bf(3 * width), bf(width), pltpu.VMEM((rows, width), F32),
             pltpu.VMEM((9, 352, 768), BF16), pltpu.VMEM((15, 224, 512), BF16),
             bf(width), bf(hidden), bf(hidden), bf(width), bf(width), bf(width),
             pltpu.VMEM((rows, width), F32), bf(3 * width),
         ],
-        compiler_params=pltpu.CompilerParams(vmem_limit_bytes=63 * 2**20),
-    )(meta, x, cot, wqkv, wout, w1, w2, vec)
+        compiler_params=pltpu.CompilerParams(vmem_limit_bytes=64 * 2**20 - 2**17),
+    )(meta, x, cot, g_attn, g_fc1, w2, g_vec)
+
+
+def bit_of(me, b):
+    return (me // (1 << b)) % 2
+
+def partner_of(me, b):
+    return me + (1 << b) * (1 - 2 * bit_of(me, b))
+
+def meet(me, bits):
+    barrier = pltpu.get_barrier_semaphore()
+    for b in range(bits):
+        pl.semaphore_signal(barrier, inc=1, device_id=(partner_of(me, b),), device_id_type=MESH)
+    pl.semaphore_wait(barrier, bits)
+
+def at_bits(ref, me, bits, free):
+    return ref.at[tuple(slice(None) if b in free else bit_of(me, b) for b in reversed(range(bits)))]
+
+
+def gather_kernel(bits, orders, *refs):
+    k = len(orders)
+    ins, outs, send, recv = refs[:k], refs[k : 2 * k], refs[2 * k], refs[2 * k + 1]
+    me = lax.axis_index("dp")
+    for i in range(k):
+        at_bits(outs[i], me, bits, ())[...] = ins[i][...]
+    meet(me, bits)
+    copies = {}
+    for stage in range(bits):
+        for i in range(k):
+            b = orders[i][stage]
+            if stage:
+                copies[i, stage - 1].wait_recv()
+            blocks = at_bits(outs[i], me, bits, orders[i][:stage])
+            c = pltpu.make_async_remote_copy(
+                src_ref=blocks, dst_ref=blocks, send_sem=send.at[i, stage], recv_sem=recv.at[i, stage],
+                device_id=(partner_of(me, b),), device_id_type=MESH)
+            c.start()
+            copies[i, stage] = c
+    for i in range(k):
+        copies[i, bits - 1].wait_recv()
+    for c in copies.values():
+        c.wait_send()
+
+
+def gather_blocks(n, orders, arrays, collective_id):
+    bits = n.bit_length() - 1
+    k = len(arrays)
+    vmem = pl.BlockSpec(memory_space=pltpu.VMEM)
+    outs = pl.pallas_call(
+        functools.partial(gather_kernel, bits, orders),
+        in_specs=[vmem] * k,
+        out_specs=[vmem] * k,
+        out_shape=[jax.ShapeDtypeStruct((2,) * bits + a.shape, a.dtype) for a in arrays],
+        scratch_shapes=[pltpu.SemaphoreType.DMA((k, bits)), pltpu.SemaphoreType.DMA((k, bits))],
+        compiler_params=pltpu.CompilerParams(collective_id=collective_id, has_side_effects=True, vmem_limit_bytes=60 * 2**20),
+    )(*arrays)
+    return [o.reshape((n,) + a.shape) for o, a in zip(outs, arrays)]
+
+
+def scatter_kernel(bits, orders, *refs):
+    k = len(orders)
+    ins, outs = refs[:k], refs[k : 2 * k]
+    rest = refs[2 * k :]
+    lands = [rest[i * bits : (i + 1) * bits] for i in range(k)]
+    rest = rest[k * bits :]
+    sums = [rest[i * (bits - 1) : (i + 1) * (bits - 1)] for i in range(k)]
+    rest = rest[k * (bits - 1) :]
+    send, recv = rest
+    me = lax.axis_index("dp")
+    meet(me, bits)
+    copies = {}
+    def idx(left, b, val):
+        return tuple(val if x == b else slice(None) for x in left)
+    def start(i, stage, src, left):
+        b = orders[i][stage]
+        mine = bit_of(me, b)
+        c = pltpu.make_async_remote_copy(
+            src_ref=src.at[idx(left, b, 1 - mine)], dst_ref=lands[i][stage], send_sem=send.at[i, stage], recv_sem=recv.at[i, stage],
+            device_id=(partner_of(me, b),), device_id_type=MESH)
+        c.start()
+        copies[i, stage] = c
+    lefts = [list(reversed(range(bits))) for _ in range(k)]
+    for i in range(k):
+        start(i, 0, ins[i], lefts[i])
+    for stage in range(bits):
+        for i in range(k):
+            b = orders[i][stage]
+            src = ins[i] if stage == 0 else sums[i][stage - 1]
+            left = lefts[i]
+            kept = src.at[idx(left, b, bit_of(me, b))]
+            copies[i, stage].wait_recv()
+            land = lands[i][stage]
+            if stage == bits - 1:
+                outs[i][...] = kept[...].astype(F32) + land[...].astype(F32)
+                continue
+            dst = sums[i][stage]
+            if len(dst.shape) == 2:
+                dst[...] = (kept[...].astype(F32) + land[...].astype(F32)).astype(dst.dtype)
+            else:
+                for t in range(2 ** (bits - 1 - stage)):
+                    at = tuple((t >> s) % 2 for s in reversed(range(bits - 1 - stage)))
+                    dst[at] = (kept[at].astype(F32) + land[at].astype(F32)).astype(dst.dtype)
+            lefts[i] = [x for x in left if x != b]
+            start(i, stage + 1, dst, lefts[i])
+    for c in copies.values():
+        c.wait_send()
+
+
+def scatter_blocks(n, orders, arrays, collective_id):
+    bits = n.bit_length() - 1
+    k = len(arrays)
+    vmem = pl.BlockSpec(memory_space=pltpu.VMEM)
+    split = [a.reshape((2,) * bits + a.shape[1:]) for a in arrays]
+    lands = [pltpu.VMEM((2,) * (bits - 1 - s) + a.shape[1:], a.dtype) for a in arrays for s in range(bits)]
+    sums = [pltpu.VMEM((2,) * (bits - 1 - s) + a.shape[1:], a.dtype) for a in arrays for s in range(bits - 1)]
+    return pl.pallas_call(
+        functools.partial(scatter_kernel, bits, orders),
+        in_specs=[vmem] * k,
+        out_specs=[vmem] * k,
+        out_shape=[jax.ShapeDtypeStruct(a.shape[1:], F32) for a in arrays],
+        scratch_shapes=lands + sums + [pltpu.SemaphoreType.DMA((k, bits)), pltpu.SemaphoreType.DMA((k, bits))],
+        compiler_params=pltpu.CompilerParams(collective_id=collective_id, has_side_effects=True, vmem_limit_bytes=60 * 2**20),
+    )(*split)
+
+
+def pieces(shard, high):
+    part, cols = shard.shape
+    folded = shard.reshape(part, 4, cols // 4).transpose(1, 0, 2).reshape(4 * part, cols // 4)
+    return jnp.pad(folded, ((0, high - 4 * part), (0, 0)))
+
+
+def unpieces(folded, part):
+    cols = folded.shape[1]
+    return folded[: 4 * part].reshape(4, part, cols).transpose(1, 0, 2).reshape(part, 4 * cols)
+
+
+def routes(bits):
+    if bits == 5:
+        return [(4, 3, 2, 1, 0), (4, 3, 1, 2, 0), (2, 1, 4, 3, 0), (4, 3, 2, 1, 0)]
+    return [tuple(reversed(range(bits)))] * 4
 
 
 def body(inputs, cotangent, w_qkv, w_out, w_fc1, w_fc2, gain1, shift1, q_bias, v_bias, out_bias, gain2, shift2,
          fc1_bias, fc2_bias, image_tokens, image_count):
-    j = lax.axis_index("dp")
+    me = lax.axis_index("dp")
     n = lax.axis_size("dp")
-    width = w_qkv.shape[1] // 3
+    part, width = w_out.shape
     hidden = w_fc1.shape[1]
-    gather = functools.partial(lax.all_gather, axis_name="dp", axis=0, tiled=True)
-    mats = [gather(w) for w in (w_qkv, w_out, w_fc1, w_fc2)]
-    small = (gain1, shift1, q_bias, v_bias, out_bias, gain2, shift2, fc2_bias)
-    packed = jnp.concatenate([jnp.stack(small).reshape(-1), fc1_bias])[None]
-    packed = gather(packed).astype(F32)
-    part = width // n
-    cols = [packed[:, i * part : (i + 1) * part].reshape(-1) for i in range(8)]
-    fc1_full = packed[:, 8 * part :].reshape(-1)
-    pad = lambda a: jnp.pad(a, (0, hidden - a.shape[0]))
-    qkv_bias = jnp.concatenate([cols[2], jnp.zeros_like(cols[2]), cols[3]])
-    vec = jnp.stack([pad(cols[0]), pad(cols[1]), pad(qkv_bias), pad(cols[4]), pad(cols[5]), pad(cols[6]), fc1_full, pad(cols[7])])
-    meta = jnp.stack([image_tokens[:, j], image_count[:, j]], axis=1)
-    out, ig, g_qkv, g_out, g_fc1, g_fc2, g_vec = layer_call(meta, inputs, cotangent, *mats, vec)
-    scatter = functools.partial(lax.psum_scatter, axis_name="dp", scatter_dimension=0, tiled=True)
-    grads = [scatter(g) for g in (g_qkv, g_out, g_fc1, g_fc2)]
-    own = [g_vec[0, :width], g_vec[1, :width], g_vec[2, :width], g_vec[2, 2 * width : 3 * width], g_vec[3, :width],
-           g_vec[4, :width], g_vec[5, :width], g_vec[7, :width]]
-    rows = jnp.concatenate([o.reshape(n, part) for o in own] + [g_vec[6].reshape(n, -1)], axis=1)
-    mine = scatter(rows)[0]
-    vs = [mine[i * part : (i + 1) * part] for i in range(8)]
-    return (out, ig, *grads, vs[0], vs[1], vs[2], vs[3], vs[4], vs[5], vs[6], mine[8 * part :], vs[7])
+    high = -(-4 * part // 16) * 16
+    orders = routes(n.bit_length() - 1)
+    small = jnp.stack([gain1, shift1, q_bias, v_bias, out_bias, gain2, shift2, fc2_bias]).astype(F32)
+    small = jnp.concatenate([
+        jnp.pad(small, ((0, 0), (0, 128 - part))),
+        jnp.pad(fc1_bias.astype(F32)[None], ((0, 7), (0, 128 - 4 * part))),
+    ])
+    attn = pieces(jnp.concatenate([w_qkv, w_out], axis=1), high)
+    fc2 = jnp.pad(w_fc2, ((0, high - 4 * part), (0, 0)))
+    g_attn, g_fc1, g_fc2, g_vec = gather_blocks(n, orders, [attn, pieces(w_fc1, high), fc2, small], 1)
+    meta = jnp.stack([
+        lax.dynamic_index_in_dim(image_tokens, me, 1, False), lax.dynamic_index_in_dim(image_count, me, 1, False)
+    ], axis=1)
+    out, ig, p_attn, p_fc1, p_fc2, p_vec = layer_call(
+        meta, inputs, cotangent, g_attn.reshape(n * high, width), g_fc1.reshape(n * high, width),
+        g_fc2[:, : 4 * part].reshape(hidden, width), g_vec)
+    p_fc2 = jnp.pad(p_fc2.reshape(n, 4 * part, width), ((0, 0), (0, high - 4 * part), (0, 0)))
+    back = [tuple(reversed(o)) for o in orders]
+    s_attn, s_fc1, s_fc2, s_vec = scatter_blocks(
+        n, back, [p_attn.reshape(n, high, width), p_fc1.reshape(n, high, width), p_fc2, p_vec], 2)
+    s_attn = unpieces(s_attn, part)
+    v = [s_vec[i, :part] for i in range(8)]
+    return (out, ig, s_attn[:, : 3 * width], s_attn[:, 3 * width :], unpieces(s_fc1, part), s_fc2[: 4 * part],
+            v[0], v[1], v[2], v[3], v[4], v[5], v[6], s_vec[8, : 4 * part], v[7])
 
 
 def solution(mesh):
-    from jax.sharding import PartitionSpec as P
     big, mat, one = P(None, "dp", None), P("dp", None), P("dp")
     return jax.shard_map(
         body, mesh=mesh,

time: 440 us -> 180 us (0.41)
  blocking collectives: 249 us -> 0 us
  Pallas kernels: 89.5 us -> 164 us
  starting transfers between devices: 61.7 us -> 0 us
  between operations: 14.4 us -> 0.73 us
  local copies, waits for them, and re-layouts: 19 us -> 10.8 us
    unnamed x3 -> x0, blocking collectives: 167 us -> none
    all_gather x2 -> x0, blocking collectives: 82.4 us -> none  [body(): mats = [gather(w) for w in (w_qkv, w_out, w_fc1, w_fc2)]]
    pallas_call x0 -> x2, Pallas kernels: none -> 66.2 us  [the longest x1 34.5 us: scatter_blocks(): pl.pallas_call(functools.partial(scatter_kernel, bits, orders), in_specs=...]
    unnamed x24 -> x0, starting transfers between devices: 61.6 us -> none
    unnamed x22 -> x7, local copies, waits for them, and re-layouts: 12.1 us -> 1.33 us
    pallas_call x1, Pallas kernels: 89.5 us -> 97.6 us  [layer_call(): pl.pallas_call(functools.partial(layer_kernel, **kw), grid=(micro,), in_s...]
  transfers between devices with their start and end apart: 27 -> 0, of which waited for: 1 -> 0; matrix products, arithmetic and copies ran while one was open for 24% -> 0% of each run, Pallas kernels for 0% -> 0%
where the time goes in v2:
time: 180 us; the launch traced here: 178 us
  Pallas kernels  164 us (91%)
  local copies, waits for them, and re-layouts  10.8 us (6%)
  other arithmetic  2.7 us (2%)
    pallas_call x1, Pallas kernels, layer_call(): pl.pallas_call(functools.partial(layer_kernel, **kw), grid=(micro,), in_s...  97.6 us
    pallas_call x1, Pallas kernels, scatter_blocks(): pl.pallas_call(functools.partial(scatter_kernel, bits, orders), in_specs=...  34.5 us
    pallas_call x1, Pallas kernels, gather_blocks(): pl.pallas_call(functools.partial(gather_kernel, bits, orders), in_specs=[...  31.7 us

profile of v2, /device:TPU:0, one launch (start us, length us, event | category | flops | bytes accessed | tf_op | source)
XLA Modules:
  0.0 178.1 jit_solution(2059754517959848873)
XLA Ops:
  0.7 0.8 stack.41
  1.4 0.8 constant_dynamic-slice_fusion
  2.2 0.7 pad_add_fusion.meta
  2.9 1.3 fusion.3.refs_3_
  4.1 0.8 reshape.67
  5.0 0.6 reshape.68.refs_1_
  5.6 0.8 pad_maximum_fusion
  6.4 0.6 reshape.66.refs_0_
  7.1 31.7 %shard_map.280 = (bf16[2,2,2,2,2,48,384]{6,5,4,3,2,1,0:T(8,128)(2,1)}, bf16[2,2,2,2,2,48,384]{6,5,4,3,2,1,0:T(8,128)(2,1)}, bf16[2,2,2,2,2,48,384]{6,5,4,3,2,1,0:T(8,128)(2,1)}, f32[2,2,2,2,2,16,128]{6,5,4,3,2,1,0:T(8,128)}) custom-call(bf16[48,384]{1,0:T(8,128)(2,1)} %reshape.66.refs_0_, bf16[48,384]{1,0:T(8,128)(2,1)} %reshape.68.refs_1_, ...), custom_call_target="tpu_custom_call" | custom-call | tf_op jit(solution)/shard_map/pallas_call | solution.py:427
  38.8 97.6 %shard_map.281 = (bf16[3,1024,384]{2,1,0:T(8,128)(2,1)}, bf16[3,1024,384]{2,1,0:T(8,128)(2,1)}, bf16[1536,384]{1,0:T(8,128)(2,1)}, bf16[1536,384]{1,0:T(8,128)(2...) custom-call(s32[3,2]{1,0:T(4,128)} %pad_add_fusion.meta, bf16[3,1024,384]{2,1,0:T(8,128)(2,1)} %x_ref.1, ...), custom_call_target="tpu_custom_call" | custom-call | tf_op jit(solution)/shard_map/pallas_call | solution.py:365
  136.4 34.5 %shard_map.282 = (f32[48,384]{1,0:T(8,128)}, f32[48,384]{1,0:T(8,128)}, f32[48,384]{1,0:T(8,128)}, f32[16,128]{1,0:T(8,128)}) custom-call(bf16[2,2,2,2,2,48,384]{6,5,4,3,2,1,0:T(8,128)(2,1)} %bitcast.52, bf16[2,2,2,2,2,48,384]{6,5,4,3,2,1,0:T(8,128)(2,1)} %bitcast.53, bf16[2,2,2,2,2,48,384]{6,5,4,3,2,1,0:T(8,128)(2,1)} %bitcast.54, ...), custom_call_target="tpu_custom_call" | custom-call | tf_op jit(solution)/shard_map/pallas_call | solution.py:494
  170.9 0.0 copy-start
  170.9 1.2 slice_bitcast_fusion.1
  172.2 1.5 slice_bitcast_fusion
  173.7 0.9 reshape.72
  174.6 0.6 slice.45
  175.2 0.6 slice.44
  175.9 0.9 reshape.74
  176.8 0.6 copy.43
  177.5 0.0 copy-done
  177.5 0.6 copy.49
  (8 shorter events, 0.2 us)
Async XLA Ops:
  170.9 6.6 %copy-start = (f32[48,384]{1,0:T(8,128)S(1)}, f32[48,384]{1,0:T(8,128)}, u32[]{:S(2)}) copy-start(f32[48,384]{1,0:T(8,128)} %get-tuple-element.73) | copy-start | bytes 221188
